TPU v7x, 32 devices: a whole 2x2x4 slice. The times are simulated.
32 devices in a mesh: group: 2 (over y), sliver: 8 (over z, x), rep: 2 (over core).
Axes of the slice: x: 2, y: 2, z: 4, core: 2. Of those that a mesh axis runs over, the one named last changes fastest.
Arguments:
- tokens: bfloat16 [64, 4096], P(('group', 'rep', 'sliver')), parts along dimension 0, may hold values from -6 to 6
- routes: int32 [64, 2], P(('group', 'rep', 'sliver')), parts along dimension 0, may hold values from 0 to 3, all different within a row
- gate_scores: int32 [64, 2], P(('group', 'rep', 'sliver')), parts along dimension 0, may hold values from 1 to 16
- gate_weight: bfloat16 [8192, 32768], P(('group', 'sliver', 'rep')), parts along dimension 0, may hold values from -0.09375 to 0.09375
- up_weight: bfloat16 [8192, 32768], P(('group', 'sliver', 'rep')), parts along dimension 0, may hold values from -0.09375 to 0.09375
- down_weight: bfloat16 [8192, 32768], P(('group', 'sliver', 'rep')), parts along dimension 0, may hold values from -0.0625 to 0.0625
Outputs:
- mixed: bfloat16 [64, 4096], P(('group', 'rep', 'sliver')), parts along dimension 0
There are 2 independent parts, one for each index of `group`. A program takes and returns all parts, laid end to end along the dimension named above; each array names one. Nothing has to cross between parts.
Inputs may be any that keep to these rules, and one draw needn't show every extreme that they name: `routes`: each row names 2 different experts.
All inputs are finite; a program needn't handle non-finite values.
Results may differ from a plain program's by a relative error of at most 0.0056.
Values may be sent and summed in bfloat16 or wider, within the bound.
No kernel may reach another device: no remote copies, remote signals or barrier semaphores. Data moves between devices by JAX's collectives and lax.ppermute only.
A program may use at most 448 MiB of HBM per device.

v0:
```python
import jax
import jax.numpy as jnp
from jax import lax
from jax.sharding import PartitionSpec as P

EXPERTS = 4


def combine_weights(routes, gate_scores, count):
    scores = gate_scores.astype(jnp.float32)
    share = scores / jnp.sum(scores, axis=1, keepdims=True)
    chosen = (routes[:, :, None] == jnp.arange(count, dtype=jnp.int32)[None, None, :]).astype(
        jnp.float32
    )
    return jnp.sum(share[:, :, None] * chosen, axis=1).astype(jnp.bfloat16)


def restore_order(stacked, slivers):
    copies, total, width = stacked.shape
    blocks = stacked.reshape(copies, slivers, total // slivers, width)
    return jnp.transpose(blocks, (1, 0, 2, 3)).reshape(copies * total, width)


def shards(tokens, routes, gate_scores, gate_weight, up_weight, down_weight):
    slivers = lax.axis_size("sliver")
    count = EXPERTS
    combine = combine_weights(routes, gate_scores, count)
    halves = (
        lax.all_to_all(gate_weight, "sliver", split_axis=1, concat_axis=0, tiled=True),
        lax.all_to_all(up_weight, "sliver", split_axis=1, concat_axis=0, tiled=True),
        lax.all_to_all(down_weight, "sliver", split_axis=1, concat_axis=0, tiled=True),
    )
    copied = (
        lax.all_gather(halves[0][None], "rep", axis=0, tiled=True),
        lax.all_gather(halves[1][None], "rep", axis=0, tiled=True),
        lax.all_gather(halves[2][None], "rep", axis=0, tiled=True),
    )
    gate_block = restore_order(copied[0], slivers)
    up_block = restore_order(copied[1], slivers)
    down_block = restore_order(copied[2], slivers)
    rows_all, combine_all = (
        lax.all_gather(tokens, "sliver", axis=0, tiled=True),
        lax.all_gather(combine, "sliver", axis=0, tiled=True),
    )
    expert_index = lax.axis_index("sliver") // (slivers // count)
    pick = (jnp.arange(count, dtype=jnp.int32) == expert_index).astype(jnp.float32)
    weight_col = jnp.sum(combine_all.astype(jnp.float32) * pick[None, :], axis=1)
    gate = jnp.dot(rows_all, gate_block, preferred_element_type=jnp.float32)
    up = jnp.dot(rows_all, up_block, preferred_element_type=jnp.float32)
    hidden = (jax.nn.silu(gate) * up * weight_col[:, None]).astype(jnp.bfloat16)
    mixed = lax.psum_scatter(
        lax.dot_general(
            hidden, down_block, (((1,), (1,)), ((), ())), preferred_element_type=jnp.float32
        ),
        "sliver",
        scatter_dimension=0,
        tiled=True,
    )
    return mixed.astype(jnp.bfloat16)


def solution(mesh):
    return jax.shard_map(
        shards,
        mesh=mesh,
        in_specs=(
            P(("group", "rep", "sliver"), None),
            P(("group", "rep", "sliver"), None),
            P(("group", "rep", "sliver"), None),
            P(("group", "sliver", "rep"), None),
            P(("group", "sliver", "rep"), None),
            P(("group", "sliver", "rep"), None),
        ),
        out_specs=P(("group", "rep", "sliver"), None),
        check_vma=False,
    )
```

profile of v0, /device:TPU:0, one launch (start us, length us, event | category | flops | bytes accessed | tf_op | source)
XLA Modules:
  0.0 1450.5 jit_solution(17940061042658535873)
XLA Ops:
  6.5 0.0 all-gather.6.cloned.1.call-start
  6.5 22.4 %copy.34 = bf16[256,32768]{0,1:T(8,128)(2,1)} copy(bf16[256,32768]{1,0:T(8,128)(2,1)} %param.9) | data formatting | bytes 33554432 | tf_op args[3]
  28.9 371.9 %all_to_all.48 = bf16[256,8,4096]{0,2,1:T(8,128)(2,1)} all-to-all(bf16[256,8,4096]{0,2,1:T(8,128)(2,1)} %bitcast.42), channel_id=1, replica_groups=mesh['group'=2,'sliver'=8,'rep'=2] {'sliver'}, dimensions={1} | all-to-all | bytes 33554432 | tf_op jit(solution)/shard_map/all_to_all | solution.py:29
  400.8 21.4 %copy.35 = bf16[8,256,4096]{2,1,0:T(8,128)(2,1)} copy(bf16[8,256,4096]{1,2,0:T(8,128)(2,1)} %bitcast.39) | data formatting | bytes 33554432 | tf_op jit(solution)/shard_map/all_to_all | solution.py:29
  422.3 0.0 all-gather.6.cloned.1.call-update
  422.3 0.0 all-gather.8.cloned.1.call-start
  422.3 24.3 %copy.37 = bf16[256,32768]{0,1:T(8,128)(2,1)} copy(bf16[256,32768]{1,0:T(8,128)(2,1)} %param.10) | data formatting | bytes 33554432 | tf_op args[4]
  446.6 368.9 %all_to_all.49 = bf16[256,8,4096]{0,2,1:T(8,128)(2,1)} all-to-all(bf16[256,8,4096]{0,2,1:T(8,128)(2,1)} %bitcast.43), channel_id=1, replica_groups=mesh['group'=2,'sliver'=8,'rep'=2] {'sliver'}, dimensions={1} | all-to-all | bytes 33554432 | tf_op jit(solution)/shard_map/all_to_all | solution.py:30
  815.5 21.3 %copy.38 = bf16[8,256,4096]{2,1,0:T(8,128)(2,1)} copy(bf16[8,256,4096]{1,2,0:T(8,128)(2,1)} %bitcast.40) | data formatting | bytes 33554432 | tf_op jit(solution)/shard_map/all_to_all | solution.py:30
  836.8 0.0 all-gather.8.cloned.1.call-update
  836.8 0.0 all-gather.10.cloned.1.call-start
  836.9 24.1 %copy.40 = bf16[256,32768]{0,1:T(8,128)(2,1)} copy(bf16[256,32768]{1,0:T(8,128)(2,1)} %param.11) | data formatting | bytes 33554432 | tf_op args[5]
  860.9 369.3 %all_to_all.50 = bf16[256,8,4096]{0,2,1:T(8,128)(2,1)} all-to-all(bf16[256,8,4096]{0,2,1:T(8,128)(2,1)} %bitcast.44), channel_id=1, replica_groups=mesh['group'=2,'sliver'=8,'rep'=2] {'sliver'}, dimensions={1} | all-to-all | bytes 33554432 | tf_op jit(solution)/shard_map/all_to_all | solution.py:31
  1230.3 0.0 copy-start
  1230.3 0.0 copy-start.3
  1230.3 0.0 copy-start.1
  1230.3 0.0 copy-start.2
  1230.3 21.2 %copy.41 = bf16[8,256,4096]{2,1,0:T(8,128)(2,1)} copy(bf16[8,256,4096]{1,2,0:T(8,128)(2,1)} %bitcast.41) | data formatting | bytes 33554432 | tf_op jit(solution)/shard_map/all_to_all | solution.py:31
  1251.5 0.0 all-gather.10.cloned.1.call-update
  1251.5 0.0 copy-done
  1251.6 30.5 %all-gather = bf16[8,2,4096]{2,1,0:T(2,128)(2,1)S(1)} all-gather(bf16[1,2,4096]{2,1,0:T(2,128)(2,1)S(1)} %bitcast.48), channel_id=1, replica_groups=mesh['group'=2,'sliver'=8,'rep'=2] {'sliver'}, dimensions={0}, use_global_device_ids=true | all-gather | bytes 147456 | tf_op jit(solution)/shard_map/all_gather | solution.py:42
  1282.1 0.1 reshape.46
  1282.2 0.0 copy-done.3
  1282.2 0.6 dynamic-slice
  1283.4 0.0 copy-done.1
  1283.4 0.1 convert_reduce_fusion
  1283.5 0.1 convert_divide_fusion
  1283.6 0.0 copy-done.2
  1283.6 0.1 fusion.11
  1283.7 18.5 %all-gather.1 = bf16[8,2,4]{2,1,0:T(2,128)(2,1)S(1)} all-gather(bf16[1,2,4]{2,1,0:T(2,128)(2,1)S(1)} %bitcast.50), channel_id=1, replica_groups=mesh['group'=2,'sliver'=8,'rep'=2] {'sliver'}, dimensions={0}, use_global_device_ids=true | all-gather | bytes 144 | tf_op jit(solution)/shard_map/all_gather | solution.py:43
  1302.3 0.1 fusion.10
  1302.4 0.0 all-gather.6.cloned.1.call-done
  1302.4 22.9 %copy.36 = bf16[8,2,256,4096]{3,2,1,0:T(8,128)(2,1)} copy(bf16[8,2,256,4096]{3,2,0,1:T(8,128)(2,1)} %bitcast.45) | data formatting | bytes 67108864 | tf_op jit(solution)/shard_map/transpose | solution.py:21
  1325.3 0.0 all-gather.8.cloned.1.call-done
  1325.3 22.7 %copy.39 = bf16[8,2,256,4096]{3,2,1,0:T(8,128)(2,1)} copy(bf16[8,2,256,4096]{3,2,0,1:T(8,128)(2,1)} %bitcast.46) | data formatting | bytes 67108864 | tf_op jit(solution)/shard_map/transpose | solution.py:21
  1348.0 0.0 all-gather.10.cloned.1.call-done
  1348.0 23.0 %copy.42 = bf16[8,2,256,4096]{3,2,1,0:T(8,128)(2,1)} copy(bf16[8,2,256,4096]{3,2,0,1:T(8,128)(2,1)} %bitcast.47) | data formatting | bytes 67108864 | tf_op jit(solution)/shard_map/transpose | solution.py:21
  1370.9 12.8 fusion.13
  1383.7 23.8 %fusion.2 = f32[16,4096]{1,0:T(8,128)S(1)} fusion(bf16[4096,4096]{1,0:T(8,128)(2,1)} %bitcast.35, bf16[16,4096]{1,0:T(8,128)(2,1)S(1)} %reshape.46, bf16[4096,4096]{1,0:T(8,128)(2,1)} %bitcast.34, f32[16,4096]{1,0:T(8,128)S(1)} %fusion.13, f32[16]{0:T(128)S(1)} %fusion.10), kind=kOutput, calls=%fused_computation.3 | convolution fusion | flops 1074200576 | bytes 67764288 | tf_op jit(solution)/shard_map/dot_general | solution.py:52
  1407.5 35.8 %all-reduce.2 = bf16[16,4096]{1,0:T(8,128)(2,1)S(1)} all-reduce(f32[16,4096]{1,0:T(8,128)S(1)} %fusion.2), channel_id=2, replica_groups=mesh['group'=2,'sliver'=8,'rep'=2] {'sliver'}, use_global_device_ids=true, to_apply=%region_3.4.clone | all-reduce | flops 65536 | bytes 393216
  1443.3 0.6 dynamic-slice_convert_fusion
  (1 shorter events, 0.0 us)
Async XLA Ops:
  6.5 1295.8 %all-gather.6.cloned.1.call-start = ((), (), s32[]{:S(2)}) async-start(), calls=%async_computation.3 | async-start | bytes 50331648 | tf_op jit(solution)/shard_map/all_gather | solution.py:34
  422.3 903.0 %all-gather.8.cloned.1.call-start = ((), (), s32[]{:S(2)}) async-start(), calls=%async_computation.4 | async-start | bytes 50331648 | tf_op jit(solution)/shard_map/all_gather | solution.py:35
  836.8 511.2 %all-gather.10.cloned.1.call-start = ((), (), s32[]{:S(2)}) async-start(), calls=%async_computation.5 | async-start | bytes 50331648 | tf_op jit(solution)/shard_map/all_gather | solution.py:36
  1230.3 21.3 %copy-start = (bf16[2,4096]{1,0:T(2,128)(2,1)S(1)}, bf16[2,4096]{1,0:T(2,128)(2,1)}, u32[]{:S(2)}) copy-start(bf16[2,4096]{1,0:T(2,128)(2,1)} %param.6) | copy-start | bytes 49156
  1230.3 51.9 %copy-start.3 = (u32[32]{0:T(128)S(1)}, u32[32]{0:T(128)}, u32[]{:S(2)}) copy-start(u32[32]{0:T(128)} %constant.31) | copy-start | bytes 388
  1230.3 53.1 %copy-start.1 = (s32[2,2]{1,0:T(2,128)S(1)}, s32[2,2]{1,0:T(2,128)}, u32[]{:S(2)}) copy-start(s32[2,2]{1,0:T(2,128)} %param.8) | copy-start | bytes 52
  1230.3 53.3 %copy-start.2 = (s32[2,2]{1,0:T(2,128)S(1)}, s32[2,2]{1,0:T(2,128)}, u32[]{:S(2)}) copy-start(s32[2,2]{1,0:T(2,128)} %param.7) | copy-start | bytes 52
Sparse Core Ops, SparseCore 0:
  422.4 50.3 all-gather.5
  836.9 50.6 all-gather.7
  1251.7 50.8 all-gather.9
where the time goes:
time: 1450 us
  blocking collectives  1200 us (83%)
  local copies, waits for them, and re-layouts  204 us (14%)
  matrix products  36.6 us (3%)
    all_to_all x1, blocking collectives, shards(): lax.all_to_all(gate_weight, 'sliver', split_axis=1, concat_axis=0, tiled=...  372 us
    all_to_all x1, blocking collectives, shards(): lax.all_to_all(down_weight, 'sliver', split_axis=1, concat_axis=0, tiled=...  369 us
    all_to_all x1, blocking collectives, shards(): lax.all_to_all(up_weight, 'sliver', split_axis=1, concat_axis=0, tiled=True)  369 us
    unnamed x13, local copies, waits for them, and re-layouts  71.4 us
    transpose x3, local copies, waits for them, and re-layouts, restore_order(): return jnp.transpose(blocks, (1, 0, 2, 3)).reshape(copies * total, width)  68.5 us
    unnamed x1, blocking collectives  35.8 us
    all_gather x1, blocking collectives, shards(): lax.all_gather(tokens, 'sliver', axis=0, tiled=True)  30.5 us
  transfers between devices with their start and end apart: 3, of which 0 were waited for; matrix products, arithmetic and copies ran while one was open for 9% of the time, Pallas kernels for 0%

commit v1 on v0

v1 whole, which is shorter than its diff:
```python
import functools

import jax
import jax.numpy as jnp
from jax import lax
from jax.experimental import pallas as pl
from jax.experimental.pallas import tpu as pltpu
from jax.sharding import PartitionSpec as P

EXPERTS = 4
TOPK = 2
PLANE = 4
EXTRA = 128
PARTS = 2
MIB = 1 << 20


def project_kernel(added, chunk, blocks_ref, rows_ref, *refs):
    weights = refs[: 2 * EXPERTS]
    extra = refs[2 * EXPERTS] if added else None
    out_ref, masked = refs[-2], refs[-1]
    count = rows_ref.shape[0]

    @pl.when((pl.program_id(0) == 0) & (pl.program_id(1) == 0))
    def _():
        rows = rows_ref[:, :chunk]
        for k in range(TOPK):
            route = rows_ref[:, chunk + k : chunk + k + 1].astype(jnp.float32)
            for e in range(EXPERTS):
                keep = (route == e).astype(jnp.float32).astype(jnp.bfloat16)
                masked[e, k * count : (k + 1) * count, :] = rows * keep

    slots, _, height, _ = out_ref.shape[1:]
    for g in range(2):
        total = jnp.zeros((TOPK * count, out_ref.shape[-1]), jnp.float32)
        for e in range(EXPERTS):
            total += jnp.dot(
                masked[e], weights[g * EXPERTS + e][...], preferred_element_type=jnp.float32
            )
        for t in range(slots):
            piece = total[t * height : (t + 1) * height]
            if added:
                piece += extra[0, t, g].astype(jnp.float32)
            out_ref[0, t, g] = piece.astype(out_ref.dtype)


def project(blocks, rows, gate_weight, up_weight, extra, slots, per_expert, kind):
    count, depth = rows.shape[0], gate_weight.shape[0]
    width = gate_weight.shape[1] // (EXPERTS * per_expert)
    cols = width // PARTS
    height = TOPK * count // slots
    steps = blocks.shape[0]

    def weight_spec(e):
        return pl.BlockSpec(
            (depth, cols), lambda i, j, b: (0, (e * per_expert + b[i]) * PARTS + j)
        )

    piece = pl.BlockSpec((1, slots, 2, height, cols), lambda i, j, b: (i, 0, 0, 0, j))
    whole = pl.BlockSpec(rows.shape, lambda i, j, b: (0, 0))
    specs = [whole] + [weight_spec(e) for e in range(EXPERTS)] * 2
    operands = [rows] + [gate_weight] * EXPERTS + [up_weight] * EXPERTS
    if extra is not None:
        specs.append(piece)
        operands.append(extra)
    shape = (steps, slots, 2, height, width)
    return pl.pallas_call(
        functools.partial(project_kernel, extra is not None, depth),
        out_shape=jax.ShapeDtypeStruct(shape, kind),
        grid_spec=pltpu.PrefetchScalarGridSpec(
            num_scalar_prefetch=1,
            grid=(steps, PARTS),
            in_specs=specs,
            out_specs=piece,
            scratch_shapes=[pltpu.VMEM((EXPERTS, TOPK * count, depth), jnp.bfloat16)],
        ),
        compiler_params=pltpu.CompilerParams(vmem_limit_bytes=40 * MIB),
        cost_estimate=pl.CostEstimate(
            flops=2 * TOPK * count * depth * width * 2 * EXPERTS * steps,
            bytes_accessed=2 * depth * width * 2 * EXPERTS * steps,
            transcendentals=0,
        ),
    )(blocks, *operands)


def mix_kernel(added, blocks_ref, routes_ref, *refs):
    hidden = refs[:PLANE]
    weights = refs[PLANE : PLANE + EXPERTS]
    extra = refs[PLANE + EXPERTS] if added else None
    out_ref, total = refs[-2], refs[-1]
    count = routes_ref.shape[0]
    cols = weights[0].shape[1]
    step, part = pl.program_id(0), pl.program_id(1)

    @pl.when((step == 0) & (part == 0))
    def _():
        total[...] = extra[...] if added else jnp.zeros_like(total)

    for d in range(PLANE):
        for j in range(PARTS):

            @pl.when((step == d) & (part == j))
            def _():
                block = hidden[d][:, j * cols : (j + 1) * cols]
                result = total[...]
                for e in range(EXPERTS):
                    first = (routes_ref[:, 0:1] == e).astype(jnp.float32).astype(jnp.bfloat16)
                    second = (routes_ref[:, 1:2] == e).astype(jnp.float32).astype(jnp.bfloat16)
                    chosen = block[:count] * first + block[count:] * second
                    result += lax.dot_general(
                        chosen,
                        weights[e][...],
                        (((1,), (1,)), ((), ())),
                        preferred_element_type=jnp.float32,
                    )
                total[...] = result

    @pl.when((step == PLANE - 1) & (part == PARTS - 1))
    def _():
        out_ref[...] = total[...].astype(out_ref.dtype)


def mix(blocks, routes, hidden, down_weight, extra, per_expert, kind):
    count, depth = routes.shape[0], down_weight.shape[0]
    width = down_weight.shape[1] // (EXPERTS * per_expert)
    cols = width // PARTS

    def weight_spec(e):
        return pl.BlockSpec(
            (depth, cols), lambda i, j, b: (0, (e * per_expert + b[i]) * PARTS + j)
        )

    def whole(shape):
        return pl.BlockSpec(shape, lambda i, j, b: (0, 0))

    specs = [whole(routes.shape)] + [whole(h.shape) for h in hidden]
    specs += [weight_spec(e) for e in range(EXPERTS)]
    operands = [routes, *hidden] + [down_weight] * EXPERTS
    if extra is not None:
        specs.append(whole(extra.shape))
        operands.append(extra)
    return pl.pallas_call(
        functools.partial(mix_kernel, extra is not None),
        out_shape=jax.ShapeDtypeStruct((count, depth), kind),
        grid_spec=pltpu.PrefetchScalarGridSpec(
            num_scalar_prefetch=1,
            grid=(PLANE, PARTS),
            in_specs=specs,
            out_specs=whole((count, depth)),
            scratch_shapes=[pltpu.VMEM((count, depth), jnp.float32)],
        ),
        compiler_params=pltpu.CompilerParams(vmem_limit_bytes=40 * MIB),
        cost_estimate=pl.CostEstimate(
            flops=2 * count * depth * width * EXPERTS * PLANE,
            bytes_accessed=2 * depth * width * EXPERTS * PLANE,
            transcendentals=0,
        ),
    )(blocks, *operands)


def shards(tokens, routes, gate_scores, gate_weight, up_weight, down_weight):
    slivers, cores = lax.axis_size("sliver"), lax.axis_size("rep")
    me, core = lax.axis_index("sliver"), lax.axis_index("rep")
    depth = gate_weight.shape[0]
    own_rows, model = tokens.shape
    devices = slivers * cores
    count = own_rows * devices
    slots = slivers // PLANE
    height = TOPK * count // slots
    per_expert = cores * PLANE

    def over_core(x):
        return lax.ppermute(x, "rep", [(i, i ^ 1) for i in range(cores)])

    def over_sliver(x, d):
        return lax.ppermute(x, "sliver", [(i, i ^ d) for i in range(slivers)])

    facts = jnp.concatenate([routes, gate_scores], axis=1).astype(jnp.bfloat16)
    facts = jnp.pad(facts, ((0, 0), (0, EXTRA - 2 * TOPK)))
    pieces = jnp.transpose(tokens.reshape(own_rows, slivers, cores, depth), (2, 1, 0, 3))
    pieces = pieces.reshape(devices, own_rows, depth)
    spread = jnp.broadcast_to(facts[None], (devices, own_rows, EXTRA))
    pieces = jnp.concatenate([pieces, spread], axis=2)
    rows = lax.all_to_all(pieces, ("rep", "sliver"), 0, 0, tiled=True)
    rows = rows.reshape(count, depth + EXTRA)
    facts = rows[:, depth : depth + 2 * TOPK].astype(jnp.float32)
    all_routes = facts[:, :TOPK]
    all_scores = facts[:, TOPK:]
    share = all_scores / jnp.sum(all_scores, axis=1, keepdims=True)
    share = share.astype(jnp.bfloat16).astype(jnp.float32).T.reshape(slots, height, 1)
    routes_padded = jnp.pad(all_routes, ((0, 0), (0, EXTRA - TOPK)))

    near = jnp.arange(PLANE, dtype=jnp.int32) ^ (me % PLANE)
    mine = core * PLANE + near
    theirs = (1 - core) * PLANE + near

    def projected(blocks, extra, kind):
        return project(
            blocks, rows, gate_weight, up_weight, extra, slots, per_expert, kind
        )

    sent = over_core(projected(theirs[1:], None, jnp.float32))
    sent_own = over_core(projected(theirs[:1], None, jnp.float32))
    chip = projected(mine[1:], sent, jnp.bfloat16)
    kept = projected(mine[:1], sent_own, jnp.float32)[0]
    arrived = [over_sliver(chip[d - 1], d) for d in range(1, PLANE)]
    terms = [kept] + arrived
    distance = slivers // 2
    while distance >= PLANE:
        bit = (me // distance) % 2
        length = terms[0].shape[0] // 2

        def part(which):
            total = 0.0
            for term in terms:
                piece = lax.dynamic_slice_in_dim(term, which * length, length, 0)
                total = total + piece.astype(jnp.float32)
            return total

        other = over_sliver(part(1 - bit).astype(jnp.bfloat16), distance)
        terms = [part(bit), other]
        distance //= 2
    total = sum(term.astype(jnp.float32) for term in terms)[0]
    weight = lax.dynamic_index_in_dim(share, me // PLANE, 0, keepdims=False)
    hidden = (jax.nn.silu(total[0]) * total[1] * weight).astype(jnp.bfloat16)

    distance = PLANE
    hidden = hidden[None]
    while distance < slivers:
        bit = (me // distance) % 2
        other = over_sliver(hidden, distance)
        hidden = jnp.where(
            bit == 0,
            jnp.concatenate([hidden, other], axis=0),
            jnp.concatenate([other, hidden], axis=0),
        )
        distance *= 2
    hidden = hidden.reshape(TOPK * count, hidden.shape[-1])
    own = [hidden] + [over_sliver(hidden, d) for d in range(1, PLANE)]
    others = [over_core(x) for x in own]
    partial = mix(mine, routes_padded, own, down_weight, None, per_expert, jnp.float32)
    mixed = mix(theirs, routes_padded, others, down_weight, partial, per_expert, jnp.bfloat16)

    pieces = mixed.reshape(devices, own_rows, depth)
    pieces = lax.all_to_all(pieces, ("rep", "sliver"), 0, 0, tiled=True)
    pieces = pieces.reshape(cores, slivers, own_rows, depth)
    return jnp.transpose(pieces, (2, 1, 0, 3)).reshape(own_rows, model)


def solution(mesh):
    return jax.shard_map(
        shards,
        mesh=mesh,
        in_specs=(
            P(("group", "rep", "sliver"), None),
            P(("group", "rep", "sliver"), None),
            P(("group", "rep", "sliver"), None),
            P(("group", "sliver", "rep"), None),
            P(("group", "sliver", "rep"), None),
            P(("group", "sliver", "rep"), None),
        ),
        out_specs=P(("group", "rep", "sliver"), None),
        check_vma=False,
    )
```

time: 1450 us -> 101 us (0.07)
  blocking collectives: 1200 us -> 9.78 us
  local copies, waits for them, and re-layouts: 204 us -> 1.65 us
  Pallas kernels: 0 us -> 38.1 us
  matrix products: 36.6 us -> 0 us
  waiting for transfers between devices: 0.06 us -> 31.7 us
  starting transfers between devices: 0.09 us -> 15.7 us
    all_to_all x3 -> x1, blocking collectives: 1110 us -> 9.78 us  [shards(): pieces = lax.all_to_all(pieces, ('rep', 'sliver'), 0, 0, tiled=True)]
    unnamed x13 -> x0, local copies, waits for them, and re-layouts: 71.4 us -> none
    transpose x3 -> x1, local copies, waits for them, and re-layouts: 68.5 us -> 0.02 us  [shards(): jnp.transpose(tokens.reshape(own_rows, slivers, cores, depth), (2, 1, 0, 3))]
    all_to_all x3 -> x0, local copies, waits for them, and re-layouts: 63.9 us -> none  [the longest x1 21.4 us: shards(): lax.all_to_all(gate_weight, 'sliver', split_axis=1, concat_axis=0, tiled=...]
    all_gather x2 -> x0, blocking collectives: 49.1 us -> none  [the longest x1 30.5 us: shards(): lax.all_gather(tokens, 'sliver', axis=0, tiled=True)]
    pallas_call x0 -> x6, Pallas kernels: none -> 38.1 us  [the longest x4 22.4 us: project(): pl.pallas_call(functools.partial(project_kernel, extra is not None, depth...]
    dot_general x2 -> x0, matrix products: 36.6 us -> none  [the longest x1 23.8 us: shards(): lax.dot_general(hidden, down_block, (((1,), (1,)), ((), ())), preferred_e...]
    unnamed x1 -> x0, blocking collectives: 35.8 us -> none
  transfers between devices with their start and end apart: 3 -> 15, of which waited for: 0 -> 9; matrix products, arithmetic and copies ran while one was open for 9% -> 1% of each run, Pallas kernels for 0% -> 22%
where the time goes in v1:
time: 101 us; the launch traced here: 99.9 us
  Pallas kernels  38.1 us (38%)
  waiting for transfers between devices  31.7 us (31%)
  starting transfers between devices  15.7 us (16%)
  blocking collectives  9.78 us (10%)
  other arithmetic  2.69 us (3%)
  local copies, waits for them, and re-layouts  1.65 us (2%)
    ppermute x8, waiting for transfers between devices, over_sliver(): return lax.ppermute(x, 'sliver', [(i, i ^ d) for i in range(slivers)])  25.3 us
    pallas_call x4, Pallas kernels, project(): pl.pallas_call(functools.partial(project_kernel, extra is not None, depth...  22.4 us
    pallas_call x2, Pallas kernels, mix(): pl.pallas_call(functools.partial(mix_kernel, extra is not None), out_shap...  15.7 us
    all_to_all x1, blocking collectives, shards(): pieces = lax.all_to_all(pieces, ('rep', 'sliver'), 0, 0, tiled=True)  9.78 us
    ppermute x8, starting transfers between devices, over_sliver(): return lax.ppermute(x, 'sliver', [(i, i ^ d) for i in range(slivers)])  7.82 us
    all_to_all x1, starting transfers between devices, shards(): rows = lax.all_to_all(pieces, ('rep', 'sliver'), 0, 0, tiled=True)  7.36 us
    all_to_all x1, waiting for transfers between devices, shards(): rows = lax.all_to_all(pieces, ('rep', 'sliver'), 0, 0, tiled=True)  6.41 us
  transfers between devices with their start and end apart: 15, of which 9 were waited for; matrix products, arithmetic and copies ran while one was open for 1% of the time, Pallas kernels for 22%

profile of v1, /device:TPU:0, one launch (start us, length us, event | category | flops | bytes accessed | tf_op | source)
XLA Modules:
  0.0 99.9 jit_solution(9837927671354744920)
XLA Ops:
  0.0 0.7 reshape.106
  0.8 0.7 convert.6
  1.4 0.7 convert.7
  2.1 0.1 fusion.12
  2.2 0.6 pad_maximum_fusion
  2.8 7.4 %all-to-all-start = ((bf16[16,2,384]{2,1,0:T(2,128)(2,1)}), bf16[16,2,384]{2,1,0:T(2,128)(2,1)S(1)}, u32[]{:S(2)}, u32[]{:S(2)}) async-start(bf16[16,2,384]{2,1,0:T(2,128)(2,1)} %pad_maximum_fusion), calls=%async_computation | async-start | bytes 49152 | tf_op jit(solution)/shard_map/all_to_all | solution.py:184
  10.2 0.1 slice.43.blocks_ref
  10.3 6.4 %all-to-all-done = bf16[16,2,384]{2,1,0:T(2,128)(2,1)S(1)} async-done(((bf16[16,2,384]{2,1,0:T(2,128)(2,1)}), bf16[16,2,384]{2,1,0:T(2,128)(2,1)S(1)}, u32[]{:S(2)}, u32[]{:S(2)}) %all-to-all-start) | async-done | bytes 24608 | tf_op jit(solution)/shard_map/all_to_all | solution.py:184
  16.7 7.9 %shard_map.66 = f32[3,2,2,32,1024]{4,3,2,1,0:T(8,128)S(1)} custom-call(s32[3]{0:T(128)S(1)} %slice.43.blocks_ref, bf16[32,384]{1,0:T(8,128)(2,1)S(1)} %reshape.108.rows_ref, bf16[256,32768]{1,0:T(8,128)(2,1)} %refs_3_.7, bf16[256,32768]{1,0:T(8,128)(2,1)} %refs_3_.7, bf16[256,32768]{1,0:T(8,128)(2,1)} %refs_3_.7, bf16[256,32768]{1,0:T(8,128)(2,1)} %refs_3_.7, ...), custom_call_target="tpu_custom_call" | custom-call | flops 805306368 | bytes 12582912 | tf_op jit(solution)/shard_map/pallas_call | solution.py:67
  24.6 0.1 collective-permute-start.1
  24.7 0.1 slice.42.blocks_ref
  24.8 3.5 %shard_map.64 = f32[1,2,2,32,1024]{4,3,2,1,0:T(8,128)} custom-call(s32[1]{0:T(128)S(1)} %bitcast.48, bf16[32,384]{1,0:T(8,128)(2,1)S(1)} %reshape.108.rows_ref, bf16[256,32768]{1,0:T(8,128)(2,1)} %refs_3_.7, bf16[256,32768]{1,0:T(8,128)(2,1)} %refs_3_.7, bf16[256,32768]{1,0:T(8,128)(2,1)} %refs_3_.7, bf16[256,32768]{1,0:T(8,128)(2,1)} %refs_3_.7, ...), custom_call_target="tpu_custom_call" | custom-call | flops 268435456 | bytes 4194304 | tf_op jit(solution)/shard_map/pallas_call | solution.py:67
  28.3 0.5 collective-permute-start
  28.8 0.0 collective-permute-done.1.refs_8_
  28.8 8.0 %shard_map.67 = bf16[3,2,2,32,1024]{4,3,2,1,0:T(8,128)(2,1)S(1)} custom-call(s32[3]{0:T(128)S(1)} %slice.42.blocks_ref, bf16[32,384]{1,0:T(8,128)(2,1)S(1)} %reshape.108.rows_ref, bf16[256,32768]{1,0:T(8,128)(2,1)} %refs_3_.7, bf16[256,32768]{1,0:T(8,128)(2,1)} %refs_3_.7, bf16[256,32768]{1,0:T(8,128)(2,1)} %refs_3_.7, bf16[256,32768]{1,0:T(8,128)(2,1)} %refs_3_.7, ...), custom_call_target="tpu_custom_call" | custom-call | flops 805306368 | bytes 12582912 | tf_op jit(solution)/shard_map/pallas_call | solution.py:67
  36.8 0.1 slice_bitcast_fusion.2
  36.9 0.6 collective-permute-start.2
  37.5 0.6 collective-permute-start.3
  38.1 2.3 %collective-permute-start.4 = (bf16[2,2,32,1024]{3,2,1,0:T(8,128)(2,1)S(1)}, bf16[2,2,32,1024]{3,2,1,0:T(8,128)(2,1)S(1)}, u32[]{:S(2)}, u32[]{:S(2)}) collective-permute-start(bf16[2,2,32,1024]{3,2,1,0:T(8,128)(2,1)S(1)} %get-tuple-element.6), channel_id=1, source_target_pairs={{0,6},{2,4},{4,2},{6,0},{8,14},{10,12},{12,10},{14,8},{1,7},{3,5},... | collective-permute-start | bytes 786440 | tf_op jit(solution)/shard_map/ppermute | solution.py:176
  40.5 0.0 collective-permute-done.refs_8_
  40.5 3.0 %shard_map.65 = f32[1,2,2,32,1024]{4,3,2,1,0:T(8,128)S(1)} custom-call(s32[1]{0:T(128)S(1)} %bitcast.49, bf16[32,384]{1,0:T(8,128)(2,1)S(1)} %reshape.108.rows_ref, bf16[256,32768]{1,0:T(8,128)(2,1)} %refs_3_.7, bf16[256,32768]{1,0:T(8,128)(2,1)} %refs_3_.7, bf16[256,32768]{1,0:T(8,128)(2,1)} %refs_3_.7, bf16[256,32768]{1,0:T(8,128)(2,1)} %refs_3_.7, ...), custom_call_target="tpu_custom_call" | custom-call | flops 268435456 | bytes 4194304 | tf_op jit(solution)/shard_map/pallas_call | solution.py:67
  43.5 1.8 %collective-permute-done.2 = bf16[2,2,32,1024]{3,2,1,0:T(8,128)(2,1)S(1)} collective-permute-done((bf16[2,2,32,1024]{3,2,1,0:T(8,128)(2,1)S(1)}, bf16[2,2,32,1024]{3,2,1,0:T(8,128)(2,1)S(1)}, u32[]{:S(2)}, u32[]{:S(2)}) %collective-permute-start.2) | collective-permute-done | bytes 262176 | tf_op jit(solution)/shard_map/ppermute | solution.py:176
  45.3 1.5 %collective-permute-done.3 = bf16[2,2,32,1024]{3,2,1,0:T(8,128)(2,1)S(1)} collective-permute-done((bf16[2,2,32,1024]{3,2,1,0:T(8,128)(2,1)S(1)}, bf16[2,2,32,1024]{3,2,1,0:T(8,128)(2,1)S(1)}, u32[]{:S(2)}, u32[]{:S(2)}) %collective-permute-start.3) | collective-permute-done | bytes 262176 | tf_op jit(solution)/shard_map/ppermute | solution.py:176
  46.7 5.3 %collective-permute-done.4 = bf16[2,2,32,1024]{3,2,1,0:T(8,128)(2,1)S(1)} collective-permute-done((bf16[2,2,32,1024]{3,2,1,0:T(8,128)(2,1)S(1)}, bf16[2,2,32,1024]{3,2,1,0:T(8,128)(2,1)S(1)}, u32[]{:S(2)}, u32[]{:S(2)}) %collective-permute-start.4) | collective-permute-done | bytes 262176 | tf_op jit(solution)/shard_map/ppermute | solution.py:176
  52.0 0.1 fusion.2
  52.1 0.7 collective-permute-start.5
  52.7 0.2 slice_reduce_fusion
  52.9 0.2 convert_reduce_fusion
  53.1 7.0 %collective-permute-done.5 = bf16[1,2,32,1024]{3,2,1,0:T(8,128)(2,1)S(1)} collective-permute-done((bf16[1,2,32,1024]{3,2,1,0:T(8,128)(2,1)S(1)}, bf16[1,2,32,1024]{3,2,1,0:T(8,128)(2,1)S(1)}, u32[]{:S(2)}, u32[]{:S(2)}) %collective-permute-start.5) | collective-permute-done | bytes 131104 | tf_op jit(solution)/shard_map/ppermute | solution.py:176
  60.1 0.1 fusion.5
  60.2 0.1 fusion.8
  60.3 0.1 collective-permute-start.6
  60.4 5.1 %collective-permute-done.6 = bf16[1,32,1024]{2,1,0:T(8,128)(2,1)S(1)} collective-permute-done((bf16[1,32,1024]{2,1,0:T(8,128)(2,1)S(1)}, bf16[1,32,1024]{2,1,0:T(8,128)(2,1)S(1)}, u32[]{:S(2)}, u32[]{:S(2)}) %collective-permute-start.6) | collective-permute-done | bytes 65568 | tf_op jit(solution)/shard_map/ppermute | solution.py:176
  65.5 0.1 collective-permute-start.10
  65.6 2.0 %collective-permute-start.12 = (bf16[64,1024]{1,0:T(8,128)(2,1)S(1)}, bf16[64,1024]{1,0:T(8,128)(2,1)S(1)}, u32[]{:S(2)}, u32[]{:S(2)}) collective-permute-start(bf16[64,1024]{1,0:T(8,128)(2,1)S(1)} %bitcast.44), channel_id=1, source_target_pairs={{0,6},{2,4},{4,2},{6,0},{8,14},{10,12},{12,10},{14,8},{1,7},{3,5},... | collective-permute-start | bytes 393224 | tf_op jit(solution)/shard_map/ppermute | solution.py:176
  67.6 1.4 %collective-permute-start.8 = (bf16[64,1024]{1,0:T(8,128)(2,1)S(1)}, bf16[64,1024]{1,0:T(8,128)(2,1)S(1)}, u32[]{:S(2)}, u32[]{:S(2)}) collective-permute-start(bf16[64,1024]{1,0:T(8,128)(2,1)S(1)} %bitcast.45), channel_id=1, source_target_pairs={{0,2},{2,0},{4,6},{6,4},{8,10},{10,8},{12,14},{14,12},{1,3},{3,1},... | collective-permute-start | bytes 393224 | tf_op jit(solution)/shard_map/ppermute | solution.py:176
  69.1 0.0 collective-permute-start.7
  69.1 1.9 %collective-permute-done.10.refs_2_ = bf16[64,1024]{1,0:T(8,128)(2,1)S(1)} collective-permute-done((bf16[64,1024]{1,0:T(8,128)(2,1)S(1)}, bf16[64,1024]{1,0:T(8,128)(2,1)S(1)}, u32[]{:S(2)}, u32[]{:S(2)}) %collective-permute-start.10) | collective-permute-done | bytes 131104 | tf_op jit(solution)/shard_map/ppermute | solution.py:176
  70.9 0.0 collective-permute-start.11
  70.9 1.5 %collective-permute-done.12.refs_3_ = bf16[64,1024]{1,0:T(8,128)(2,1)S(1)} collective-permute-done((bf16[64,1024]{1,0:T(8,128)(2,1)S(1)}, bf16[64,1024]{1,0:T(8,128)(2,1)S(1)}, u32[]{:S(2)}, u32[]{:S(2)}) %collective-permute-start.12) | collective-permute-done | bytes 131104 | tf_op jit(solution)/shard_map/ppermute | solution.py:176
  72.4 0.0 collective-permute-start.13
  72.4 1.3 %collective-permute-done.8.refs_1_ = bf16[64,1024]{1,0:T(8,128)(2,1)S(1)} collective-permute-done((bf16[64,1024]{1,0:T(8,128)(2,1)S(1)}, bf16[64,1024]{1,0:T(8,128)(2,1)S(1)}, u32[]{:S(2)}, u32[]{:S(2)}) %collective-permute-start.8) | collective-permute-done | bytes 131104 | tf_op jit(solution)/shard_map/ppermute | solution.py:176
  73.7 0.0 collective-permute-start.9
  73.7 7.8 %shard_map.68.refs_8_ = f32[32,256]{1,0:T(8,128)S(1)} custom-call(s32[4]{0:T(128)S(1)} %fusion.13.blocks_ref, f32[32,128]{1,0:T(8,128)S(1)} %pad.9.routes_ref, bf16[64,1024]{1,0:T(8,128)(2,1)S(1)} %bitcast.47, bf16[64,1024]{1,0:T(8,128)(2,1)S(1)} %collective-permute-done.8.refs_1_, bf16[64,1024]{1,0:T(8,128)(2,1)S(1)} %collective-permute-done.10.refs_2_, ...), custom_call_target="tpu_custom_call" | custom-call | flops 268435456 | bytes 8388608 | tf_op jit(solution)/shard_map/pallas_call | solution.py:142
  81.6 0.0 collective-permute-done.7.refs_0_
  81.6 0.0 collective-permute-done.11.refs_2_
  81.6 0.0 collective-permute-done.13.refs_3_
  81.6 0.0 collective-permute-done.9.refs_1_
  81.6 7.8 %shard_map.69 = bf16[32,256]{1,0:T(8,128)(2,1)S(1)} custom-call(s32[4]{0:T(128)S(1)} %fusion.14.blocks_ref, f32[32,128]{1,0:T(8,128)S(1)} %pad.9.routes_ref, bf16[64,1024]{1,0:T(8,128)(2,1)S(1)} %collective-permute-done.7.refs_0_, bf16[64,1024]{1,0:T(8,128)(2,1)S(1)} %collective-permute-done.9.refs_1_, bf16[64,1024]{1,0:T(8,128)(2,1)S(1)} %collective-permute-done.11.refs_2_, ...), custom_call_target="tpu_custom_call" | custom-call | flops 268435456 | bytes 8388608 | tf_op jit(solution)/shard_map/pallas_call | solution.py:142
  89.5 9.8 %all_to_all.10 = bf16[16,2,256]{2,1,0:T(2,128)(2,1)S(1)} all-to-all(bf16[16,2,256]{2,1,0:T(2,128)(2,1)S(1)} %reshape.109), channel_id=1, replica_groups=mesh['group'=2,'sliver'=8,'rep'=2] {'rep','sliver'}, dimensions={0} | all-to-all | bytes 32768 | tf_op jit(solution)/shard_map/all_to_all | solution.py:245
  99.3 0.6 reshape.111
  (10 shorter events, 0.1 us)
Async XLA Ops:
  2.8 13.9 %all-to-all-start = ((bf16[16,2,384]{2,1,0:T(2,128)(2,1)}), bf16[16,2,384]{2,1,0:T(2,128)(2,1)S(1)}, u32[]{:S(2)}, u32[]{:S(2)}) async-start(bf16[16,2,384]{2,1,0:T(2,128)(2,1)} %pad_maximum_fusion), calls=%async_computation | async-start | bytes 49152 | tf_op jit(solution)/shard_map/all_to_all | solution.py:184
  24.6 4.2 %collective-permute-start.1 = (f32[3,2,2,32,1024]{4,3,2,1,0:T(8,128)S(1)}, f32[3,2,2,32,1024]{4,3,2,1,0:T(8,128)S(1)}, u32[]{:S(2)}, u32[]{:S(2)}) collective-permute-start(f32[3,2,2,32,1024]{4,3,2,1,0:T(8,128)S(1)} %shard_map.66), channel_id=1, source_target_pairs={{0,1},{1,0},{2,3},{3,2},{4,5},{5,4},{6,7},{7,6},{8,9},{9,8},{10,11... | collective-permute-start | bytes 4718600 | tf_op jit(solution)/shard_map/ppermute | solution.py:173
  28.3 12.1 %collective-permute-start = (f32[1,2,2,32,1024]{4,3,2,1,0:T(8,128)}, f32[1,2,2,32,1024]{4,3,2,1,0:T(8,128)}, u32[]{:S(2)}, u32[]{:S(2)}) collective-permute-start(f32[1,2,2,32,1024]{4,3,2,1,0:T(8,128)} %shard_map.64), channel_id=1, source_target_pairs={{0,1},{1,0},{2,3},{3,2},{4,5},{5,4},{6,7},{7,6},{8,9},{9,8},{10,11... | collective-permute-start | bytes 1572872 | tf_op jit(solution)/shard_map/ppermute | solution.py:173
  36.9 8.4 %collective-permute-start.2 = (bf16[2,2,32,1024]{3,2,1,0:T(8,128)(2,1)S(1)}, bf16[2,2,32,1024]{3,2,1,0:T(8,128)(2,1)S(1)}, u32[]{:S(2)}, u32[]{:S(2)}) collective-permute-start(bf16[2,2,32,1024]{3,2,1,0:T(8,128)(2,1)S(1)} %get-tuple-element.5), channel_id=1, source_target_pairs={{0,2},{2,0},{4,6},{6,4},{8,10},{10,8},{12,14},{14,12},{1,3},{3,1},... | collective-permute-start | bytes 786440 | tf_op jit(solution)/shard_map/ppermute | solution.py:176
  37.5 9.2 %collective-permute-start.3 = (bf16[2,2,32,1024]{3,2,1,0:T(8,128)(2,1)S(1)}, bf16[2,2,32,1024]{3,2,1,0:T(8,128)(2,1)S(1)}, u32[]{:S(2)}, u32[]{:S(2)}) collective-permute-start(bf16[2,2,32,1024]{3,2,1,0:T(8,128)(2,1)S(1)} %get-tuple-element.7), channel_id=1, source_target_pairs={{0,4},{2,6},{4,0},{6,2},{8,12},{10,14},{12,8},{14,10},{1,5},{3,7},... | collective-permute-start | bytes 786440 | tf_op jit(solution)/shard_map/ppermute | solution.py:176
  38.1 13.9 %collective-permute-start.4 = (bf16[2,2,32,1024]{3,2,1,0:T(8,128)(2,1)S(1)}, bf16[2,2,32,1024]{3,2,1,0:T(8,128)(2,1)S(1)}, u32[]{:S(2)}, u32[]{:S(2)}) collective-permute-start(bf16[2,2,32,1024]{3,2,1,0:T(8,128)(2,1)S(1)} %get-tuple-element.6), channel_id=1, source_target_pairs={{0,6},{2,4},{4,2},{6,0},{8,14},{10,12},{12,10},{14,8},{1,7},{3,5},... | collective-permute-start | bytes 786440 | tf_op jit(solution)/shard_map/ppermute | solution.py:176
  52.1 8.0 %collective-permute-start.5 = (bf16[1,2,32,1024]{3,2,1,0:T(8,128)(2,1)S(1)}, bf16[1,2,32,1024]{3,2,1,0:T(8,128)(2,1)S(1)}, u32[]{:S(2)}, u32[]{:S(2)}) collective-permute-start(bf16[1,2,32,1024]{3,2,1,0:T(8,128)(2,1)S(1)} %fusion.2), channel_id=1, source_target_pairs={{0,8},{2,10},{4,12},{6,14},{8,0},{10,2},{12,4},{14,6},{1,9},{3,11}... | collective-permute-start | bytes 393224 | tf_op jit(solution)/shard_map/ppermute | solution.py:176
  60.3 5.2 %collective-permute-start.6 = (bf16[1,32,1024]{2,1,0:T(8,128)(2,1)S(1)}, bf16[1,32,1024]{2,1,0:T(8,128)(2,1)S(1)}, u32[]{:S(2)}, u32[]{:S(2)}) collective-permute-start(bf16[1,32,1024]{2,1,0:T(8,128)(2,1)S(1)} %fusion.8), channel_id=1, source_target_pairs={{0,8},{2,10},{4,12},{6,14},{8,0},{10,2},{12,4},{14,6},{1,9},{3,11}... | collective-permute-start | bytes 196616 | tf_op jit(solution)/shard_map/ppermute | solution.py:176
  65.5 5.4 %collective-permute-start.10 = (bf16[64,1024]{1,0:T(8,128)(2,1)S(1)}, bf16[64,1024]{1,0:T(8,128)(2,1)S(1)}, u32[]{:S(2)}, u32[]{:S(2)}) collective-permute-start(bf16[64,1024]{1,0:T(8,128)(2,1)S(1)} %bitcast.43), channel_id=1, source_target_pairs={{0,4},{2,6},{4,0},{6,2},{8,12},{10,14},{12,8},{14,10},{1,5},{3,7},... | collective-permute-start | bytes 393224 | tf_op jit(solution)/shard_map/ppermute | solution.py:176
  65.6 6.8 %collective-permute-start.12 = (bf16[64,1024]{1,0:T(8,128)(2,1)S(1)}, bf16[64,1024]{1,0:T(8,128)(2,1)S(1)}, u32[]{:S(2)}, u32[]{:S(2)}) collective-permute-start(bf16[64,1024]{1,0:T(8,128)(2,1)S(1)} %bitcast.44), channel_id=1, source_target_pairs={{0,6},{2,4},{4,2},{6,0},{8,14},{10,12},{12,10},{14,8},{1,7},{3,5},... | collective-permute-start | bytes 393224 | tf_op jit(solution)/shard_map/ppermute | solution.py:176
  67.6 6.1 %collective-permute-start.8 = (bf16[64,1024]{1,0:T(8,128)(2,1)S(1)}, bf16[64,1024]{1,0:T(8,128)(2,1)S(1)}, u32[]{:S(2)}, u32[]{:S(2)}) collective-permute-start(bf16[64,1024]{1,0:T(8,128)(2,1)S(1)} %bitcast.45), channel_id=1, source_target_pairs={{0,2},{2,0},{4,6},{6,4},{8,10},{10,8},{12,14},{14,12},{1,3},{3,1},... | collective-permute-start | bytes 393224 | tf_op jit(solution)/shard_map/ppermute | solution.py:176
  69.1 12.5 %collective-permute-start.7 = (bf16[64,1024]{1,0:T(8,128)(2,1)S(1)}, bf16[64,1024]{1,0:T(8,128)(2,1)S(1)}, u32[]{:S(2)}, u32[]{:S(2)}) collective-permute-start(bf16[64,1024]{1,0:T(8,128)(2,1)S(1)} %bitcast.46), channel_id=1, source_target_pairs={{0,1},{1,0},{2,3},{3,2},{4,5},{5,4},{6,7},{7,6},{8,9},{9,8},{10,11... | collective-permute-start | bytes 393224 | tf_op jit(solution)/shard_map/ppermute | solution.py:173
  70.9 10.7 %collective-permute-start.11 = (bf16[64,1024]{1,0:T(8,128)(2,1)S(1)}, bf16[64,1024]{1,0:T(8,128)(2,1)S(1)}, u32[]{:S(2)}, u32[]{:S(2)}) collective-permute-start(bf16[64,1024]{1,0:T(8,128)(2,1)S(1)} %collective-permute-done.10.refs_2_), channel_id=1, source_target_pairs={{0,1},{1,0},{2,3},{3,2},{4,5},{5,4},{6,7},{7,6},{8,9},{9,8},{10,11... | collective-permute-start | bytes 393224 | tf_op jit(solution)/shard_map/ppermute | solution.py:173
  72.4 9.2 %collective-permute-start.13 = (bf16[64,1024]{1,0:T(8,128)(2,1)S(1)}, bf16[64,1024]{1,0:T(8,128)(2,1)S(1)}, u32[]{:S(2)}, u32[]{:S(2)}) collective-permute-start(bf16[64,1024]{1,0:T(8,128)(2,1)S(1)} %collective-permute-done.12.refs_3_), channel_id=1, source_target_pairs={{0,1},{1,0},{2,3},{3,2},{4,5},{5,4},{6,7},{7,6},{8,9},{9,8},{10,11... | collective-permute-start | bytes 393224 | tf_op jit(solution)/shard_map/ppermute | solution.py:173
  73.7 7.9 %collective-permute-start.9 = (bf16[64,1024]{1,0:T(8,128)(2,1)S(1)}, bf16[64,1024]{1,0:T(8,128)(2,1)S(1)}, u32[]{:S(2)}, u32[]{:S(2)}) collective-permute-start(bf16[64,1024]{1,0:T(8,128)(2,1)S(1)} %collective-permute-done.8.refs_1_), channel_id=1, source_target_pairs={{0,1},{1,0},{2,3},{3,2},{4,5},{5,4},{6,7},{7,6},{8,9},{9,8},{10,11... | collective-permute-start | bytes 393224 | tf_op jit(solution)/shard_map/ppermute | solution.py:173

commit v2 on v0

v2 whole, which is shorter than its diff:
```python
import functools

import jax
import jax.numpy as jnp
from jax import lax
from jax.experimental import pallas as pl
from jax.experimental.pallas import tpu as pltpu
from jax.sharding import PartitionSpec as P

EXPERTS = 4
TOPK = 2
PLANE = 4
EXTRA = 128
CHUNKS = 1
MIB = 1 << 20
ANY = pl.BlockSpec(memory_space=pl.ANY)
VMEM = pl.BlockSpec(memory_space=pltpu.VMEM)
SMEM = pl.BlockSpec(memory_space=pltpu.SMEM)


def in_hbm(x):
    return pltpu.with_memory_space_constraint(x, pltpu.HBM)


def limit(*sizes):
    return pltpu.CompilerParams(vmem_limit_bytes=min(sum(sizes) + 6 * MIB, 60 * MIB))


def pack_kernel(tokens_ref, routes_ref, scores_ref, out_ref):
    devices, own_rows, width = out_ref.shape
    depth = width - EXTRA
    cores = 2
    slivers = devices // cores
    lane = lax.broadcasted_iota(jnp.int32, (own_rows, EXTRA), 1)
    facts = jnp.zeros((own_rows, EXTRA), jnp.int32)
    for k in range(TOPK):
        facts = jnp.where(lane == k, routes_ref[:, k : k + 1], facts)
        facts = jnp.where(lane == TOPK + k, scores_ref[:, k : k + 1], facts)
    facts = facts.astype(jnp.float32).astype(out_ref.dtype)
    for r in range(cores):
        for s in range(slivers):
            first = (s * cores + r) * depth
            out_ref[r * slivers + s, :, :depth] = tokens_ref[:, first : first + depth]
            out_ref[r * slivers + s, :, depth:] = facts


def packed(tokens, routes, gate_scores, slivers, cores, depth):
    own_rows = tokens.shape[0]
    devices = slivers * cores
    if depth % 128 == 0 and cores == 2:
        return pl.pallas_call(
            pack_kernel,
            out_shape=jax.ShapeDtypeStruct((devices, own_rows, depth + EXTRA), tokens.dtype),
            in_specs=[VMEM] * 3,
            out_specs=VMEM,
        )(tokens, routes, gate_scores)
    facts = jnp.concatenate([routes, gate_scores], axis=1).astype(tokens.dtype)
    facts = jnp.pad(facts, ((0, 0), (0, EXTRA - 2 * TOPK)))
    pieces = jnp.transpose(tokens.reshape(own_rows, slivers, cores, depth), (2, 1, 0, 3))
    pieces = pieces.reshape(devices, own_rows, depth)
    spread = jnp.broadcast_to(facts[None], (devices, own_rows, EXTRA))
    return jnp.concatenate([pieces, spread], axis=2)


def after(x, *before):
    return lax.optimization_barrier((x, *before))[0]


def project_kernel(blocks_ref, rows_ref, gate_ref, up_ref, *refs):
    outs, (masked, buffer, sems) = refs[:-3], refs[-3:]
    places = [(out, i) for out in outs for i in range(out.shape[0])]
    steps = len(places)
    _, slots, _, height, cols = outs[0].shape
    depth = gate_ref.shape[0]
    count = rows_ref.shape[0]
    per_expert = gate_ref.shape[1] // (EXPERTS * cols)
    copies = []
    for i in range(steps):
        for g, ref in enumerate((gate_ref, up_ref)):
            for e in range(EXPERTS):
                first = pl.multiple_of((e * per_expert + blocks_ref[i]) * cols, cols)
                copies.append(
                    pltpu.make_async_copy(
                        ref.at[:, pl.ds(first, cols)],
                        buffer.at[i, g, pl.ds(e * depth, depth)],
                        sems.at[i, g, e],
                    )
                )
                copies[-1].start()
    rows = rows_ref[:, :depth]
    for k in range(TOPK):
        route = rows_ref[:, depth + k : depth + k + 1].astype(jnp.float32)
        for e in range(EXPERTS):
            keep = (route == e).astype(jnp.float32).astype(jnp.bfloat16)
            masked[k * count : (k + 1) * count, e * depth : (e + 1) * depth] = rows * keep
    for i in range(steps):
        for g in range(2):
            for e in range(EXPERTS):
                copies[(i * 2 + g) * EXPERTS + e].wait()
            total = jnp.dot(masked[...], buffer[i, g], preferred_element_type=jnp.float32)
            out, at = places[i]
            out[at, :, g] = total.reshape(slots, height, cols).astype(out.dtype)


def project(blocks, splits, kinds, rows, gate_weight, up_weight, slots, width):
    depth = gate_weight.shape[0]
    pairs = TOPK * rows.shape[0]
    steps = sum(splits)
    shapes = [(n, slots, 2, pairs // slots, width) for n in splits]
    weights = steps * 2 * EXPERTS * depth * width
    return pl.pallas_call(
        project_kernel,
        out_shape=[jax.ShapeDtypeStruct(s, k) for s, k in zip(shapes, kinds)],
        in_specs=[SMEM, VMEM, ANY, ANY],
        out_specs=[VMEM] * len(splits),
        scratch_shapes=[
            pltpu.VMEM((pairs, EXPERTS * depth), jnp.bfloat16),
            pltpu.VMEM((steps, 2, EXPERTS * depth, width), jnp.bfloat16),
            pltpu.SemaphoreType.DMA((steps, 2, EXPERTS)),
        ],
        compiler_params=limit(2 * weights, 8 * steps * pairs * width),
        cost_estimate=pl.CostEstimate(
            flops=2 * pairs * weights, bytes_accessed=2 * weights, transcendentals=0
        ),
    )(blocks, rows, in_hbm(gate_weight), in_hbm(up_weight))


def mix_kernel(steps, added, blocks_ref, routes_ref, *refs):
    hidden, refs = refs[:steps], refs[steps:]
    down_ref, refs = refs[0], refs[1:]
    extra = refs[0] if added else None
    out_ref, stacked, buffer, sems = refs[-4:]
    count, depth = out_ref.shape
    cols = hidden[0].shape[1]
    per_expert = down_ref.shape[1] // (EXPERTS * cols)
    copies = []
    for i in range(steps):
        for e in range(EXPERTS):
            first = pl.multiple_of((e * per_expert + blocks_ref[i]) * cols, cols)
            copies.append(
                pltpu.make_async_copy(
                    down_ref.at[:, pl.ds(first, cols)],
                    buffer.at[i, e],
                    sems.at[i, e],
                )
            )
            copies[-1].start()
    masks = [
        [(routes_ref[:, k : k + 1] == e).astype(jnp.float32) for k in range(TOPK)]
        for e in range(EXPERTS)
    ]
    for e in range(EXPERTS):
        keep = [jnp.broadcast_to(m, (count, cols)).astype(jnp.bfloat16) for m in masks[e]]
        for i in range(steps):
            stacked[i, e] = sum(hidden[i][k * count : (k + 1) * count] * keep[k] for k in range(TOPK))

    def step(i, total):
        for e in range(EXPERTS):
            pltpu.make_async_copy(buffer.at[i, e], buffer.at[i, e], sems.at[i, e]).wait()
        for e in range(EXPERTS):
            total += lax.dot_general(
                stacked[i, e],
                buffer[i, e],
                (((1,), (1,)), ((), ())),
                preferred_element_type=jnp.float32,
            )
        return total

    total = extra[...] if added else jnp.zeros((count, depth), jnp.float32)
    total = lax.fori_loop(0, steps, step, total)
    out_ref[...] = total.astype(out_ref.dtype)


def mix(blocks, routes, hidden, down_weight, extra, kind):
    count, depth = routes.shape[0], down_weight.shape[0]
    width = hidden[0].shape[1]
    steps = len(hidden)
    room = 16 * steps * count * width
    if room > 32 * MIB and steps > 1:
        part = steps // 2
        extra = mix(blocks[:part], routes, hidden[:part], down_weight, extra, jnp.float32)
        return mix(blocks[part:], routes, hidden[part:], down_weight, extra, kind)
    weights = steps * EXPERTS * depth * width
    operands = [blocks, routes, *hidden, in_hbm(down_weight)]
    specs = [SMEM] + [VMEM] * (1 + steps) + [ANY]
    if extra is not None:
        operands.append(extra)
        specs.append(VMEM)
    return pl.pallas_call(
        functools.partial(mix_kernel, steps, extra is not None),
        out_shape=jax.ShapeDtypeStruct((count, depth), kind),
        in_specs=specs,
        out_specs=VMEM,
        scratch_shapes=[
            pltpu.VMEM((steps, EXPERTS, count, width), jnp.bfloat16),
            pltpu.VMEM((steps, EXPERTS, depth, width), jnp.bfloat16),
            pltpu.SemaphoreType.DMA((steps, EXPERTS)),
        ],
        compiler_params=limit(2 * weights, room),
        cost_estimate=pl.CostEstimate(
            flops=2 * count * weights, bytes_accessed=2 * weights, transcendentals=0
        ),
    )(*operands)


def shards(tokens, routes, gate_scores, gate_weight, up_weight, down_weight):
    slivers, cores = lax.axis_size("sliver"), lax.axis_size("rep")
    me, core = lax.axis_index("sliver"), lax.axis_index("rep")
    depth, columns = gate_weight.shape
    own_rows, model = tokens.shape
    devices = slivers * cores
    count = own_rows * devices
    slots = slivers // PLANE
    height = TOPK * count // slots
    width = columns // (EXPERTS * cores * PLANE * CHUNKS)

    def over_core(x):
        return lax.ppermute(x, "rep", [(i, i ^ 1) for i in range(cores)])

    def over_sliver(x, d):
        return lax.ppermute(x, "sliver", [(i, i ^ d) for i in range(slivers)])

    pieces = packed(tokens, routes, gate_scores, slivers, cores, depth)
    rows = lax.all_to_all(pieces, ("rep", "sliver"), 0, 0, tiled=True)
    rows = rows.reshape(count, depth + EXTRA)
    facts = rows[:, depth : depth + 2 * TOPK].astype(jnp.float32)
    all_routes = facts[:, :TOPK]
    all_scores = facts[:, TOPK:]
    share = all_scores / jnp.sum(all_scores, axis=1, keepdims=True)
    share = share.astype(jnp.bfloat16).astype(jnp.float32).T.reshape(slots, height, 1)
    weight = lax.dynamic_index_in_dim(share, me // PLANE, 0, keepdims=False)
    routes_padded = jnp.pad(all_routes, ((0, 0), (0, EXTRA - TOPK)))

    near = jnp.arange(PLANE, dtype=jnp.int32) ^ (me % PLANE)
    mine = (core * PLANE + near) * CHUNKS
    theirs = ((1 - core) * PLANE + near) * CHUNKS

    def projected(blocks, splits, kinds=(jnp.float32,)):
        return project(blocks, splits, kinds, rows, gate_weight, up_weight, slots, width)

    far, far_own = projected(
        jnp.concatenate([theirs[1:], theirs[:1]]), (PLANE - 1, 1), (jnp.float32, jnp.bfloat16)
    )
    far, far_own = over_core(far), over_core(far_own)
    (chip,) = projected(mine[1:], (PLANE - 1,))
    chip = (chip + far).astype(jnp.bfloat16)
    (kept,) = projected(after(mine[:1], chip), (1,))
    halves = 2 if slots > 1 else 1
    top = me // (slivers // 2) if halves == 2 else 0
    length = slots // halves

    def half(x, which):
        return lax.dynamic_slice_in_dim(x, which * length, length, 0)

    terms = []
    for which in [1 - top, top][2 - halves :]:
        sent = [half(chip[d - 1], which) for d in range(1, PLANE)]
        arrived = [over_sliver(sent[d - 1], d) for d in range(1, PLANE)]
        terms.append(arrived + [half(kept[0], which), half(far_own[0], which)])

    def summed(terms):
        return sum(term.astype(jnp.float32) for term in terms)

    gathered = []
    for c in range(CHUNKS):
        distance = slivers // 2
        parts = terms[-1]
        if halves == 2:
            parts = parts + [over_sliver(summed(terms[0]).astype(jnp.bfloat16), distance)]
            distance //= 2
        while distance >= PLANE:
            bit = (me // distance) % 2
            length = parts[0].shape[0] // 2

            def part(which):
                return summed(
                    [lax.dynamic_slice_in_dim(x, which * length, length, 0) for x in parts]
                )

            other = over_sliver(part(1 - bit).astype(jnp.bfloat16), distance)
            parts = [part(bit), other]
            distance //= 2
        total = sum(term.astype(jnp.float32) for term in parts)[0]
        hidden = (jax.nn.silu(total[0]) * total[1] * weight).astype(jnp.bfloat16)[None]
        distance = PLANE
        while distance < slivers:
            bit = (me // distance) % 2
            other = over_sliver(hidden, distance)
            hidden = jnp.where(
                bit == 0,
                jnp.concatenate([hidden, other], axis=0),
                jnp.concatenate([other, hidden], axis=0),
            )
            distance *= 2
        hidden = hidden.reshape(TOPK * count, width)
        gathered.append([hidden] + [over_sliver(hidden, d) for d in range(1, PLANE)])

    (gathered,) = gathered
    order = jnp.stack([mine[0], theirs[0]])
    first = [gathered[0], over_core(gathered[0])]
    mixed = mix(order, routes_padded, first, down_weight, None, jnp.float32)
    rest = [after(x, mixed) for x in gathered[1:]]
    rest_other = [over_core(x) for x in rest]
    order = jnp.concatenate([mine[1:], theirs[1:]])
    mixed = mix(order, routes_padded, rest + rest_other, down_weight, mixed, jnp.bfloat16)

    pieces = mixed.reshape(devices, own_rows, depth)
    pieces = lax.all_to_all(pieces, ("rep", "sliver"), 0, 0, tiled=True)
    pieces = pieces.reshape(cores, slivers, own_rows, depth)
    return jnp.transpose(pieces, (2, 1, 0, 3)).reshape(own_rows, model)


def solution(mesh):
    return jax.shard_map(
        shards,
        mesh=mesh,
        in_specs=(
            P(("group", "rep", "sliver"), None),
            P(("group", "rep", "sliver"), None),
            P(("group", "rep", "sliver"), None),
            P(("group", "sliver", "rep"), None),
            P(("group", "sliver", "rep"), None),
            P(("group", "sliver", "rep"), None),
        ),
        out_specs=P(("group", "rep", "sliver"), None),
        check_vma=False,
    )
```

time: 1450 us -> 80.8 us (0.06)
  blocking collectives: 1200 us -> 9.11 us
  local copies, waits for them, and re-layouts: 204 us -> 0.95 us
  matrix products: 36.6 us -> 0 us
  Pallas kernels: 0 us -> 27.5 us
  waiting for transfers between devices: 0.06 us -> 20.7 us
  starting transfers between devices: 0.09 us -> 20.7 us
    all_to_all x3 -> x1, blocking collectives: 1110 us -> 9.11 us  [shards(): pieces = lax.all_to_all(pieces, ('rep', 'sliver'), 0, 0, tiled=True)]
    unnamed x13 -> x0, local copies, waits for them, and re-layouts: 71.4 us -> none
    transpose x3 -> x0, local copies, waits for them, and re-layouts: 68.5 us -> none  [restore_order(): return jnp.transpose(blocks, (1, 0, 2, 3)).reshape(copies * total, width)]
    all_to_all x3 -> x0, local copies, waits for them, and re-layouts: 63.9 us -> none  [the longest x1 21.4 us: shards(): lax.all_to_all(gate_weight, 'sliver', split_axis=1, concat_axis=0, tiled=...]
    all_gather x2 -> x0, blocking collectives: 49.1 us -> none  [the longest x1 30.5 us: shards(): lax.all_gather(tokens, 'sliver', axis=0, tiled=True)]
    dot_general x2 -> x0, matrix products: 36.6 us -> none  [the longest x1 23.8 us: shards(): lax.dot_general(hidden, down_block, (((1,), (1,)), ((), ())), preferred_e...]
    unnamed x1 -> x0, blocking collectives: 35.8 us -> none
    pallas_call x0 -> x6, Pallas kernels: none -> 27.5 us  [the longest x3 15.7 us: project(): pl.pallas_call(project_kernel, out_shape=[jax.ShapeDtypeStruct(s, k) for...]
  transfers between devices with their start and end apart: 3 -> 18, of which waited for: 0 -> 9; matrix products, arithmetic and copies ran while one was open for 9% -> 2% of each run, Pallas kernels for 0% -> 15%
where the time goes in v2:
time: 80.8 us; the launch traced here: 80.5 us
  Pallas kernels  27.5 us (34%)
  starting transfers between devices  20.7 us (26%)
  waiting for transfers between devices  20.7 us (26%)
  blocking collectives  9.11 us (11%)
  other arithmetic  1.31 us (2%)
  local copies, waits for them, and re-layouts  0.95 us (1%)
    pallas_call x3, Pallas kernels, project(): pl.pallas_call(project_kernel, out_shape=[jax.ShapeDtypeStruct(s, k) for...  15.7 us
    ppermute x11, waiting for transfers between devices, over_sliver(): return lax.ppermute(x, 'sliver', [(i, i ^ d) for i in range(slivers)])  13.2 us
    ppermute x11, starting transfers between devices, over_sliver(): return lax.ppermute(x, 'sliver', [(i, i ^ d) for i in range(slivers)])  12.6 us
    pallas_call x2, Pallas kernels, mix(): pl.pallas_call(functools.partial(mix_kernel, steps, extra is not None), o...  10.3 us
    all_to_all x1, blocking collectives, shards(): pieces = lax.all_to_all(pieces, ('rep', 'sliver'), 0, 0, tiled=True)  9.11 us
    all_to_all x1, starting transfers between devices, shards(): rows = lax.all_to_all(pieces, ('rep', 'sliver'), 0, 0, tiled=True)  7.36 us
    all_to_all x1, waiting for transfers between devices, shards(): rows = lax.all_to_all(pieces, ('rep', 'sliver'), 0, 0, tiled=True)  6.3 us
  transfers between devices with their start and end apart: 18, of which 9 were waited for; matrix products, arithmetic and copies ran while one was open for 2% of the time, Pallas kernels for 15%

profile of v2, /device:TPU:0, one launch (start us, length us, event | category | flops | bytes accessed | tf_op | source)
XLA Modules:
  0.0 80.5 jit_solution(6582823707181229931)
XLA Ops:
  0.0 1.4 %shard_map.64 = bf16[16,2,384]{2,1,0:T(2,128)(2,1)} custom-call(bf16[2,4096]{1,0:T(2,128)(2,1)} %tokens_ref.1, s32[2,2]{1,0:T(2,128)} %routes_ref.1, s32[2,2]{1,0:T(2,128)} %scores_ref.1), custom_call_target="tpu_custom_call" | custom-call | tf_op jit(solution)/shard_map/pallas_call | solution.py:51
  1.4 7.4 %all-to-all-start = ((bf16[16,2,384]{2,1,0:T(2,128)(2,1)}), bf16[16,2,384]{2,1,0:T(2,128)(2,1)S(1)}, u32[]{:S(2)}, u32[]{:S(2)}) async-start(bf16[16,2,384]{2,1,0:T(2,128)(2,1)} %shard_map.64), calls=%async_computation | async-start | bytes 49152 | tf_op jit(solution)/shard_map/all_to_all | solution.py:224
  8.8 0.1 slice.46
  8.9 0.1 pad_add_fusion.1.blocks_ref
  9.0 6.3 %all-to-all-done = bf16[16,2,384]{2,1,0:T(2,128)(2,1)S(1)} async-done(((bf16[16,2,384]{2,1,0:T(2,128)(2,1)}), bf16[16,2,384]{2,1,0:T(2,128)(2,1)S(1)}, u32[]{:S(2)}, u32[]{:S(2)}) %all-to-all-start) | async-done | bytes 24608 | tf_op jit(solution)/shard_map/all_to_all | solution.py:224
  15.3 7.1 %shard_map.66 = (f32[3,2,2,32,1024]{4,3,2,1,0:T(8,128)S(1)}, bf16[1,2,2,32,1024]{4,3,2,1,0:T(8,128)(2,1)S(1)}) custom-call(s32[4]{0:T(128)S(1)} %pad_add_fusion.1.blocks_ref, bf16[32,384]{1,0:T(8,128)(2,1)S(1)} %reshape.135.rows_ref, bf16[256,32768]{1,0:T(8,128)(2,1)} %gate_ref.5, bf16[256,32768]{1,0:T(8,128)(2,1)} %up_ref.5), custom_call_target="tpu_custom_call" | custom-call | flops 1073741824 | bytes 16777216 | tf_op jit(solution)/shard_map/pallas_call | solution.py:111
  22.5 0.1 collective-permute-start
  22.6 0.1 slice.45.blocks_ref
  22.7 0.5 collective-permute-start.4
  23.1 5.9 %shard_map.65 = f32[3,2,2,32,1024]{4,3,2,1,0:T(8,128)S(1)} custom-call(s32[3]{0:T(128)S(1)} %slice.45.blocks_ref, bf16[32,384]{1,0:T(8,128)(2,1)S(1)} %reshape.135.rows_ref, bf16[256,32768]{1,0:T(8,128)(2,1)} %gate_ref.5, bf16[256,32768]{1,0:T(8,128)(2,1)} %up_ref.5), custom_call_target="tpu_custom_call" | custom-call | flops 805306368 | bytes 12582912 | tf_op jit(solution)/shard_map/pallas_call | solution.py:111
  29.0 0.0 collective-permute-done
  29.0 0.4 add_convert_fusion
  29.4 0.1 fusion.8
  29.5 0.6 collective-permute-start.5
  30.1 0.6 collective-permute-start.6
  30.8 2.4 %collective-permute-start.7 = (bf16[1,2,32,1024]{3,2,1,0:T(8,128)(2,1)S(1)}, bf16[1,2,32,1024]{3,2,1,0:T(8,128)(2,1)S(1)}, u32[]{:S(2)}, u32[]{:S(2)}) collective-permute-start(bf16[1,2,32,1024]{3,2,1,0:T(8,128)(2,1)S(1)} %get-tuple-element.25), channel_id=1, source_target_pairs={{0,6},{2,4},{4,2},{6,0},{8,14},{10,12},{12,10},{14,8},{1,7},{3,5},... | collective-permute-start | bytes 393224 | tf_op jit(solution)/shard_map/ppermute | solution.py:221
  33.2 0.6 collective-permute-start.1
  33.8 2.7 %shard_map.67 = f32[1,2,2,32,1024]{4,3,2,1,0:T(8,128)S(1)} custom-call(s32[1]{0:T(128)S(1)} %bitcast.50, bf16[32,384]{1,0:T(8,128)(2,1)S(1)} %reshape.135.rows_ref, bf16[256,32768]{1,0:T(8,128)(2,1)} %gate_ref.5, bf16[256,32768]{1,0:T(8,128)(2,1)} %up_ref.5), custom_call_target="tpu_custom_call" | custom-call | flops 268435456 | bytes 4194304 | tf_op jit(solution)/shard_map/pallas_call | solution.py:111
  36.5 0.0 collective-permute-done.4
  36.5 0.6 collective-permute-start.2
  37.2 0.0 collective-permute-done.5
  37.2 2.3 %collective-permute-start.3 = (bf16[1,2,32,1024]{3,2,1,0:T(8,128)(2,1)S(1)}, bf16[1,2,32,1024]{3,2,1,0:T(8,128)(2,1)S(1)}, u32[]{:S(2)}, u32[]{:S(2)}) collective-permute-start(bf16[1,2,32,1024]{3,2,1,0:T(8,128)(2,1)S(1)} %get-tuple-element.24), channel_id=1, source_target_pairs={{0,6},{2,4},{4,2},{6,0},{8,14},{10,12},{12,10},{14,8},{1,7},{3,5},... | collective-permute-start | bytes 393224 | tf_op jit(solution)/shard_map/ppermute | solution.py:221
  39.5 0.0 collective-permute-done.6
  39.5 0.0 collective-permute-done.7
  39.6 0.1 fusion
  39.6 0.7 collective-permute-start.8
  40.3 0.2 slice_reduce_fusion
  40.5 0.2 convert_reduce_fusion
  40.7 0.6 collective-permute-done.1
  41.3 2.4 %collective-permute-done.2 = bf16[1,2,32,1024]{3,2,1,0:T(8,128)(2,1)S(1)} collective-permute-done((bf16[1,2,32,1024]{3,2,1,0:T(8,128)(2,1)S(1)}, bf16[1,2,32,1024]{3,2,1,0:T(8,128)(2,1)S(1)}, u32[]{:S(2)}, u32[]{:S(2)}) %collective-permute-start.2) | collective-permute-done | bytes 131104 | tf_op jit(solution)/shard_map/ppermute | solution.py:221
  43.7 3.9 %collective-permute-done.3 = bf16[1,2,32,1024]{3,2,1,0:T(8,128)(2,1)S(1)} collective-permute-done((bf16[1,2,32,1024]{3,2,1,0:T(8,128)(2,1)S(1)}, bf16[1,2,32,1024]{3,2,1,0:T(8,128)(2,1)S(1)}, u32[]{:S(2)}, u32[]{:S(2)}) %collective-permute-start.3) | collective-permute-done | bytes 131104 | tf_op jit(solution)/shard_map/ppermute | solution.py:221
  47.6 0.0 collective-permute-done.8
  47.6 0.1 fusion.1
  47.7 0.1 fusion.4
  47.7 1.2 %collective-permute-start.9 = (bf16[1,32,1024]{2,1,0:T(8,128)(2,1)S(1)}, bf16[1,32,1024]{2,1,0:T(8,128)(2,1)S(1)}, u32[]{:S(2)}, u32[]{:S(2)}) collective-permute-start(bf16[1,32,1024]{2,1,0:T(8,128)(2,1)S(1)} %fusion.4), channel_id=1, source_target_pairs={{0,8},{2,10},{4,12},{6,14},{8,0},{10,2},{12,4},{14,6},{1,9},{3,11}... | collective-permute-start | bytes 196616 | tf_op jit(solution)/shard_map/ppermute | solution.py:221
  48.9 4.0 %collective-permute-done.9 = bf16[1,32,1024]{2,1,0:T(8,128)(2,1)S(1)} collective-permute-done((bf16[1,32,1024]{2,1,0:T(8,128)(2,1)S(1)}, bf16[1,32,1024]{2,1,0:T(8,128)(2,1)S(1)}, u32[]{:S(2)}, u32[]{:S(2)}) %collective-permute-start.9) | collective-permute-done | bytes 65568 | tf_op jit(solution)/shard_map/ppermute | solution.py:221
  53.0 0.1 collective-permute-start.11
  53.1 0.8 %collective-permute-start.13 = (bf16[64,1024]{1,0:T(8,128)(2,1)S(1)}, bf16[64,1024]{1,0:T(8,128)(2,1)S(1)}, u32[]{:S(2)}, u32[]{:S(2)}) collective-permute-start(bf16[64,1024]{1,0:T(8,128)(2,1)S(1)} %bitcast.46), channel_id=1, source_target_pairs={{0,6},{2,4},{4,2},{6,0},{8,14},{10,12},{12,10},{14,8},{1,7},{3,5},... | collective-permute-start | bytes 393224 | tf_op jit(solution)/shard_map/ppermute | solution.py:221
  53.9 1.6 %collective-permute-start.12 = (bf16[64,1024]{1,0:T(8,128)(2,1)S(1)}, bf16[64,1024]{1,0:T(8,128)(2,1)S(1)}, u32[]{:S(2)}, u32[]{:S(2)}) collective-permute-start(bf16[64,1024]{1,0:T(8,128)(2,1)S(1)} %bitcast.47), channel_id=1, source_target_pairs={{0,4},{2,6},{4,0},{6,2},{8,12},{10,14},{12,8},{14,10},{1,5},{3,7},... | collective-permute-start | bytes 393224 | tf_op jit(solution)/shard_map/ppermute | solution.py:221
  55.5 1.1 %collective-permute-start.10 = (bf16[64,1024]{1,0:T(8,128)(2,1)S(1)}, bf16[64,1024]{1,0:T(8,128)(2,1)S(1)}, u32[]{:S(2)}, u32[]{:S(2)}) collective-permute-start(bf16[64,1024]{1,0:T(8,128)(2,1)S(1)} %bitcast.48), channel_id=1, source_target_pairs={{0,2},{2,0},{4,6},{6,4},{8,10},{10,8},{12,14},{14,12},{1,3},{3,1},... | collective-permute-start | bytes 393224 | tf_op jit(solution)/shard_map/ppermute | solution.py:221
  56.6 0.1 pad_add_fusion.2.blocks_ref
  56.7 0.0 collective-permute-done.11.refs_1_
  56.7 3.6 %shard_map.68.refs_7_ = f32[32,256]{1,0:T(8,128)S(1)} custom-call(s32[2]{0:T(128)S(1)} %pad_add_fusion.2.blocks_ref, f32[32,128]{1,0:T(8,128)S(1)} %pad.4.routes_ref, bf16[64,1024]{1,0:T(8,128)(2,1)S(1)} %bitcast.49, bf16[64,1024]{1,0:T(8,128)(2,1)S(1)} %collective-permute-done.11.refs_1_, bf16[256,32768]{1,0:T(8,128)(2,1)} %refs_6_.1), custom_call_target="tpu_custom_call" | custom-call | flops 134217728 | bytes 4194304 | tf_op jit(solution)/shard_map/pallas_call | solution.py:189
  60.4 0.0 collective-permute-done.13.refs_2_
  60.4 0.1 collective-permute-start.16
  60.4 1.7 %collective-permute-done.12.refs_1_ = bf16[64,1024]{1,0:T(8,128)(2,1)S(1)} collective-permute-done((bf16[64,1024]{1,0:T(8,128)(2,1)S(1)}, bf16[64,1024]{1,0:T(8,128)(2,1)S(1)}, u32[]{:S(2)}, u32[]{:S(2)}) %collective-permute-start.12) | collective-permute-done | bytes 131104 | tf_op jit(solution)/shard_map/ppermute | solution.py:221
  62.1 0.0 collective-permute-start.15
  62.1 0.6 collective-permute-done.10.refs_0_
  62.7 0.0 collective-permute-start.14
  62.7 0.1 pad_add_fusion.blocks_ref
  62.8 0.0 collective-permute-done.16.refs_5_
  62.8 0.7 collective-permute-done.15.refs_4_
  63.5 0.6 collective-permute-done.14.refs_3_
  64.0 6.7 %shard_map.69 = bf16[32,256]{1,0:T(8,128)(2,1)S(1)} custom-call(s32[6]{0:T(128)S(1)} %pad_add_fusion.blocks_ref, f32[32,128]{1,0:T(8,128)S(1)} %pad.4.routes_ref, bf16[64,1024]{1,0:T(8,128)(2,1)S(1)} %collective-permute-done.10.refs_0_, bf16[64,1024]{1,0:T(8,128)(2,1)S(1)} %collective-permute-done.12.refs_1_, ...), custom_call_target="tpu_custom_call" | custom-call | flops 402653184 | bytes 12582912 | tf_op jit(solution)/shard_map/pallas_call | solution.py:189
  70.8 9.1 %all_to_all.10 = bf16[16,2,256]{2,1,0:T(2,128)(2,1)S(1)} all-to-all(bf16[16,2,256]{2,1,0:T(2,128)(2,1)S(1)} %reshape.136), channel_id=1, replica_groups=mesh['group'=2,'sliver'=8,'rep'=2] {'rep','sliver'}, dimensions={0} | all-to-all | bytes 32768 | tf_op jit(solution)/shard_map/all_to_all | solution.py:308
  79.9 0.6 reshape.138
  (11 shorter events, 0.1 us)
Async XLA Ops:
  1.4 13.9 %all-to-all-start = ((bf16[16,2,384]{2,1,0:T(2,128)(2,1)}), bf16[16,2,384]{2,1,0:T(2,128)(2,1)S(1)}, u32[]{:S(2)}, u32[]{:S(2)}) async-start(bf16[16,2,384]{2,1,0:T(2,128)(2,1)} %shard_map.64), calls=%async_computation | async-start | bytes 49152 | tf_op jit(solution)/shard_map/all_to_all | solution.py:224
  22.5 6.5 %collective-permute-start = (f32[3,2,2,32,1024]{4,3,2,1,0:T(8,128)S(1)}, f32[3,2,2,32,1024]{4,3,2,1,0:T(8,128)S(1)}, u32[]{:S(2)}, u32[]{:S(2)}) collective-permute-start(f32[3,2,2,32,1024]{4,3,2,1,0:T(8,128)S(1)} %get-tuple-element.11), channel_id=1, source_target_pairs={{0,1},{1,0},{2,3},{3,2},{4,5},{5,4},{6,7},{7,6},{8,9},{9,8},{10,11... | collective-permute-start | bytes 4718600 | tf_op jit(solution)/shard_map/ppermute | solution.py:218
  22.7 13.9 %collective-permute-start.4 = (bf16[1,2,2,32,1024]{4,3,2,1,0:T(8,128)(2,1)S(1)}, bf16[1,2,2,32,1024]{4,3,2,1,0:T(8,128)(2,1)S(1)}, u32[]{:S(2)}, u32[]{:S(2)}) collective-permute-start(bf16[1,2,2,32,1024]{4,3,2,1,0:T(8,128)(2,1)S(1)} %get-tuple-element.13), channel_id=1, source_target_pairs={{0,1},{1,0},{2,3},{3,2},{4,5},{5,4},{6,7},{7,6},{8,9},{9,8},{10,11... | collective-permute-start | bytes 786440 | tf_op jit(solution)/shard_map/ppermute | solution.py:218
  29.5 7.7 %collective-permute-start.5 = (bf16[1,2,32,1024]{3,2,1,0:T(8,128)(2,1)S(1)}, bf16[1,2,32,1024]{3,2,1,0:T(8,128)(2,1)S(1)}, u32[]{:S(2)}, u32[]{:S(2)}) collective-permute-start(bf16[1,2,32,1024]{3,2,1,0:T(8,128)(2,1)S(1)} %get-tuple-element.21), channel_id=1, source_target_pairs={{0,2},{2,0},{4,6},{6,4},{8,10},{10,8},{12,14},{14,12},{1,3},{3,1},... | collective-permute-start | bytes 393224 | tf_op jit(solution)/shard_map/ppermute | solution.py:221
  30.1 9.4 %collective-permute-start.6 = (bf16[1,2,32,1024]{3,2,1,0:T(8,128)(2,1)S(1)}, bf16[1,2,32,1024]{3,2,1,0:T(8,128)(2,1)S(1)}, u32[]{:S(2)}, u32[]{:S(2)}) collective-permute-start(bf16[1,2,32,1024]{3,2,1,0:T(8,128)(2,1)S(1)} %get-tuple-element.23), channel_id=1, source_target_pairs={{0,4},{2,6},{4,0},{6,2},{8,12},{10,14},{12,8},{14,10},{1,5},{3,7},... | collective-permute-start | bytes 393224 | tf_op jit(solution)/shard_map/ppermute | solution.py:221
  30.8 8.7 %collective-permute-start.7 = (bf16[1,2,32,1024]{3,2,1,0:T(8,128)(2,1)S(1)}, bf16[1,2,32,1024]{3,2,1,0:T(8,128)(2,1)S(1)}, u32[]{:S(2)}, u32[]{:S(2)}) collective-permute-start(bf16[1,2,32,1024]{3,2,1,0:T(8,128)(2,1)S(1)} %get-tuple-element.25), channel_id=1, source_target_pairs={{0,6},{2,4},{4,2},{6,0},{8,14},{10,12},{12,10},{14,8},{1,7},{3,5},... | collective-permute-start | bytes 393224 | tf_op jit(solution)/shard_map/ppermute | solution.py:221
  33.2 8.1 %collective-permute-start.1 = (bf16[1,2,32,1024]{3,2,1,0:T(8,128)(2,1)S(1)}, bf16[1,2,32,1024]{3,2,1,0:T(8,128)(2,1)S(1)}, u32[]{:S(2)}, u32[]{:S(2)}) collective-permute-start(bf16[1,2,32,1024]{3,2,1,0:T(8,128)(2,1)S(1)} %get-tuple-element.20), channel_id=1, source_target_pairs={{0,2},{2,0},{4,6},{6,4},{8,10},{10,8},{12,14},{14,12},{1,3},{3,1},... | collective-permute-start | bytes 393224 | tf_op jit(solution)/shard_map/ppermute | solution.py:221
  36.5 7.1 %collective-permute-start.2 = (bf16[1,2,32,1024]{3,2,1,0:T(8,128)(2,1)S(1)}, bf16[1,2,32,1024]{3,2,1,0:T(8,128)(2,1)S(1)}, u32[]{:S(2)}, u32[]{:S(2)}) collective-permute-start(bf16[1,2,32,1024]{3,2,1,0:T(8,128)(2,1)S(1)} %get-tuple-element.22), channel_id=1, source_target_pairs={{0,4},{2,6},{4,0},{6,2},{8,12},{10,14},{12,8},{14,10},{1,5},{3,7},... | collective-permute-start | bytes 393224 | tf_op jit(solution)/shard_map/ppermute | solution.py:221
  37.2 10.4 %collective-permute-start.3 = (bf16[1,2,32,1024]{3,2,1,0:T(8,128)(2,1)S(1)}, bf16[1,2,32,1024]{3,2,1,0:T(8,128)(2,1)S(1)}, u32[]{:S(2)}, u32[]{:S(2)}) collective-permute-start(bf16[1,2,32,1024]{3,2,1,0:T(8,128)(2,1)S(1)} %get-tuple-element.24), channel_id=1, source_target_pairs={{0,6},{2,4},{4,2},{6,0},{8,14},{10,12},{12,10},{14,8},{1,7},{3,5},... | collective-permute-start | bytes 393224 | tf_op jit(solution)/shard_map/ppermute | solution.py:221
  39.6 7.9 %collective-permute-start.8 = (bf16[1,2,32,1024]{3,2,1,0:T(8,128)(2,1)S(1)}, bf16[1,2,32,1024]{3,2,1,0:T(8,128)(2,1)S(1)}, u32[]{:S(2)}, u32[]{:S(2)}) collective-permute-start(bf16[1,2,32,1024]{3,2,1,0:T(8,128)(2,1)S(1)} %fusion), channel_id=1, source_target_pairs={{0,8},{2,10},{4,12},{6,14},{8,0},{10,2},{12,4},{14,6},{1,9},{3,11}... | collective-permute-start | bytes 393224 | tf_op jit(solution)/shard_map/ppermute | solution.py:221
  47.7 5.2 %collective-permute-start.9 = (bf16[1,32,1024]{2,1,0:T(8,128)(2,1)S(1)}, bf16[1,32,1024]{2,1,0:T(8,128)(2,1)S(1)}, u32[]{:S(2)}, u32[]{:S(2)}) collective-permute-start(bf16[1,32,1024]{2,1,0:T(8,128)(2,1)S(1)} %fusion.4), channel_id=1, source_target_pairs={{0,8},{2,10},{4,12},{6,14},{8,0},{10,2},{12,4},{14,6},{1,9},{3,11}... | collective-permute-start | bytes 196616 | tf_op jit(solution)/shard_map/ppermute | solution.py:221
  53.0 3.8 %collective-permute-start.11 = (bf16[64,1024]{1,0:T(8,128)(2,1)S(1)}, bf16[64,1024]{1,0:T(8,128)(2,1)S(1)}, u32[]{:S(2)}, u32[]{:S(2)}) collective-permute-start(bf16[64,1024]{1,0:T(8,128)(2,1)S(1)} %bitcast.45), channel_id=1, source_target_pairs={{0,1},{1,0},{2,3},{3,2},{4,5},{5,4},{6,7},{7,6},{8,9},{9,8},{10,11... | collective-permute-start | bytes 393224 | tf_op jit(solution)/shard_map/ppermute | solution.py:218
  53.1 7.3 %collective-permute-start.13 = (bf16[64,1024]{1,0:T(8,128)(2,1)S(1)}, bf16[64,1024]{1,0:T(8,128)(2,1)S(1)}, u32[]{:S(2)}, u32[]{:S(2)}) collective-permute-start(bf16[64,1024]{1,0:T(8,128)(2,1)S(1)} %bitcast.46), channel_id=1, source_target_pairs={{0,6},{2,4},{4,2},{6,0},{8,14},{10,12},{12,10},{14,8},{1,7},{3,5},... | collective-permute-start | bytes 393224 | tf_op jit(solution)/shard_map/ppermute | solution.py:221
  53.9 8.2 %collective-permute-start.12 = (bf16[64,1024]{1,0:T(8,128)(2,1)S(1)}, bf16[64,1024]{1,0:T(8,128)(2,1)S(1)}, u32[]{:S(2)}, u32[]{:S(2)}) collective-permute-start(bf16[64,1024]{1,0:T(8,128)(2,1)S(1)} %bitcast.47), channel_id=1, source_target_pairs={{0,4},{2,6},{4,0},{6,2},{8,12},{10,14},{12,8},{14,10},{1,5},{3,7},... | collective-permute-start | bytes 393224 | tf_op jit(solution)/shard_map/ppermute | solution.py:221
  55.5 7.2 %collective-permute-start.10 = (bf16[64,1024]{1,0:T(8,128)(2,1)S(1)}, bf16[64,1024]{1,0:T(8,128)(2,1)S(1)}, u32[]{:S(2)}, u32[]{:S(2)}) collective-permute-start(bf16[64,1024]{1,0:T(8,128)(2,1)S(1)} %bitcast.48), channel_id=1, source_target_pairs={{0,2},{2,0},{4,6},{6,4},{8,10},{10,8},{12,14},{14,12},{1,3},{3,1},... | collective-permute-start | bytes 393224 | tf_op jit(solution)/shard_map/ppermute | solution.py:221
  60.4 2.4 %collective-permute-start.16 = (bf16[64,1024]{1,0:T(8,128)(2,1)S(1)}, bf16[64,1024]{1,0:T(8,128)(2,1)S(1)}, u32[]{:S(2)}, u32[]{:S(2)}) collective-permute-start(bf16[64,1024]{1,0:T(8,128)(2,1)S(1)} %collective-permute-done.13.refs_2_), channel_id=1, source_target_pairs={{0,1},{1,0},{2,3},{3,2},{4,5},{5,4},{6,7},{7,6},{8,9},{9,8},{10,11... | collective-permute-start | bytes 393224 | tf_op jit(solution)/shard_map/ppermute | solution.py:218
  62.1 1.3 %collective-permute-start.15 = (bf16[64,1024]{1,0:T(8,128)(2,1)S(1)}, bf16[64,1024]{1,0:T(8,128)(2,1)S(1)}, u32[]{:S(2)}, u32[]{:S(2)}) collective-permute-start(bf16[64,1024]{1,0:T(8,128)(2,1)S(1)} %collective-permute-done.12.refs_1_), channel_id=1, source_target_pairs={{0,1},{1,0},{2,3},{3,2},{4,5},{5,4},{6,7},{7,6},{8,9},{9,8},{10,11... | collective-permute-start | bytes 393224 | tf_op jit(solution)/shard_map/ppermute | solution.py:218
  62.7 1.3 %collective-permute-start.14 = (bf16[64,1024]{1,0:T(8,128)(2,1)S(1)}, bf16[64,1024]{1,0:T(8,128)(2,1)S(1)}, u32[]{:S(2)}, u32[]{:S(2)}) collective-permute-start(bf16[64,1024]{1,0:T(8,128)(2,1)S(1)} %collective-permute-done.10.refs_0_), channel_id=1, source_target_pairs={{0,1},{1,0},{2,3},{3,2},{4,5},{5,4},{6,7},{7,6},{8,9},{9,8},{10,11... | collective-permute-start | bytes 393224 | tf_op jit(solution)/shard_map/ppermute | solution.py:218

commit v3 on v2

--- a/solution.py
+++ b/solution.py
@@ -15,7 +15,6 @@
 MIB = 1 << 20
 ANY = pl.BlockSpec(memory_space=pl.ANY)
 VMEM = pl.BlockSpec(memory_space=pltpu.VMEM)
-SMEM = pl.BlockSpec(memory_space=pltpu.SMEM)
 
 
 def in_hbm(x):
@@ -26,7 +25,16 @@
     return pltpu.CompilerParams(vmem_limit_bytes=min(sum(sizes) + 6 * MIB, 60 * MIB))
 
 
-def pack_kernel(tokens_ref, routes_ref, scores_ref, out_ref):
+def pack_kernel(tokens_hbm, routes_hbm, scores_hbm, out_ref, *scratch):
+    tokens_ref, routes_ref, scores_ref, sems = scratch
+    copies = [
+        pltpu.make_async_copy(source, target, sems.at[i])
+        for i, (source, target) in enumerate(zip((tokens_hbm, routes_hbm, scores_hbm), scratch))
+    ]
+    for copy in copies:
+        copy.start()
+    for copy in copies:
+        copy.wait()
     devices, own_rows, width = out_ref.shape
     depth = width - EXTRA
     cores = 2
@@ -50,10 +58,14 @@
     if depth % 128 == 0 and cores == 2:
         return pl.pallas_call(
             pack_kernel,
-            out_shape=jax.ShapeDtypeStruct((devices, own_rows, depth + EXTRA), tokens.dtype),
-            in_specs=[VMEM] * 3,
+            out_shape=pltpu.MemorySpace.VMEM((devices, own_rows, depth + EXTRA), tokens.dtype),
+            in_specs=[ANY] * 3,
             out_specs=VMEM,
-        )(tokens, routes, gate_scores)
+            scratch_shapes=[
+                *[pltpu.VMEM(x.shape, x.dtype) for x in (tokens, routes, gate_scores)],
+                pltpu.SemaphoreType.DMA((3,)),
+            ],
+        )(in_hbm(tokens), in_hbm(routes), in_hbm(gate_scores))
     facts = jnp.concatenate([routes, gate_scores], axis=1).astype(tokens.dtype)
     facts = jnp.pad(facts, ((0, 0), (0, EXTRA - 2 * TOPK)))
     pieces = jnp.transpose(tokens.reshape(own_rows, slivers, cores, depth), (2, 1, 0, 3))
@@ -66,7 +78,17 @@
     return lax.optimization_barrier((x, *before))[0]
 
 
-def project_kernel(blocks_ref, rows_ref, gate_ref, up_ref, *refs):
+def own_block(d):
+    return lax.axis_index("rep") * PLANE + lax.bitwise_xor(lax.axis_index("sliver") % PLANE, d)
+
+
+def other_block(d):
+    return PLANE - lax.axis_index("rep") * PLANE + lax.bitwise_xor(
+        lax.axis_index("sliver") % PLANE, d
+    )
+
+
+def project_kernel(blocks, rows_ref, gate_ref, up_ref, *refs):
     outs, (masked, buffer, sems) = refs[:-3], refs[-3:]
     places = [(out, i) for out in outs for i in range(out.shape[0])]
     steps = len(places)
@@ -75,10 +97,11 @@
     count = rows_ref.shape[0]
     per_expert = gate_ref.shape[1] // (EXPERTS * cols)
     copies = []
-    for i in range(steps):
+    for i, (where, d) in enumerate(blocks):
+        block = where(d)
         for g, ref in enumerate((gate_ref, up_ref)):
             for e in range(EXPERTS):
-                first = pl.multiple_of((e * per_expert + blocks_ref[i]) * cols, cols)
+                first = pl.multiple_of((e * per_expert + block) * cols, cols)
                 copies.append(
                     pltpu.make_async_copy(
                         ref.at[:, pl.ds(first, cols)],
@@ -109,9 +132,9 @@
     shapes = [(n, slots, 2, pairs // slots, width) for n in splits]
     weights = steps * 2 * EXPERTS * depth * width
     return pl.pallas_call(
-        project_kernel,
+        functools.partial(project_kernel, blocks),
         out_shape=[jax.ShapeDtypeStruct(s, k) for s, k in zip(shapes, kinds)],
-        in_specs=[SMEM, VMEM, ANY, ANY],
+        in_specs=[VMEM, ANY, ANY],
         out_specs=[VMEM] * len(splits),
         scratch_shapes=[
             pltpu.VMEM((pairs, EXPERTS * depth), jnp.bfloat16),
@@ -122,10 +145,11 @@
         cost_estimate=pl.CostEstimate(
             flops=2 * pairs * weights, bytes_accessed=2 * weights, transcendentals=0
         ),
-    )(blocks, rows, in_hbm(gate_weight), in_hbm(up_weight))
-
-
-def mix_kernel(steps, added, blocks_ref, routes_ref, *refs):
+    )(rows, in_hbm(gate_weight), in_hbm(up_weight))
+
+
+def mix_kernel(blocks, added, routes_ref, *refs):
+    steps = len(blocks)
     hidden, refs = refs[:steps], refs[steps:]
     down_ref, refs = refs[0], refs[1:]
     extra = refs[0] if added else None
@@ -134,9 +158,10 @@
     cols = hidden[0].shape[1]
     per_expert = down_ref.shape[1] // (EXPERTS * cols)
     copies = []
-    for i in range(steps):
+    for i, (where, d) in enumerate(blocks):
+        block = where(d)
         for e in range(EXPERTS):
-            first = pl.multiple_of((e * per_expert + blocks_ref[i]) * cols, cols)
+            first = pl.multiple_of((e * per_expert + block) * cols, cols)
             copies.append(
                 pltpu.make_async_copy(
                     down_ref.at[:, pl.ds(first, cols)],
@@ -181,13 +206,13 @@
         extra = mix(blocks[:part], routes, hidden[:part], down_weight, extra, jnp.float32)
         return mix(blocks[part:], routes, hidden[part:], down_weight, extra, kind)
     weights = steps * EXPERTS * depth * width
-    operands = [blocks, routes, *hidden, in_hbm(down_weight)]
-    specs = [SMEM] + [VMEM] * (1 + steps) + [ANY]
+    operands = [routes, *hidden, in_hbm(down_weight)]
+    specs = [VMEM] * (1 + steps) + [ANY]
     if extra is not None:
         operands.append(extra)
         specs.append(VMEM)
     return pl.pallas_call(
-        functools.partial(mix_kernel, steps, extra is not None),
+        functools.partial(mix_kernel, blocks, extra is not None),
         out_shape=jax.ShapeDtypeStruct((count, depth), kind),
         in_specs=specs,
         out_specs=VMEM,
@@ -231,20 +256,20 @@
     weight = lax.dynamic_index_in_dim(share, me // PLANE, 0, keepdims=False)
     routes_padded = jnp.pad(all_routes, ((0, 0), (0, EXTRA - TOPK)))
 
-    near = jnp.arange(PLANE, dtype=jnp.int32) ^ (me % PLANE)
-    mine = (core * PLANE + near) * CHUNKS
-    theirs = ((1 - core) * PLANE + near) * CHUNKS
-
-    def projected(blocks, splits, kinds=(jnp.float32,)):
-        return project(blocks, splits, kinds, rows, gate_weight, up_weight, slots, width)
+    mine = [(own_block, d) for d in range(PLANE)]
+    theirs = [(other_block, d) for d in range(PLANE)]
+
+    def projected(blocks, splits, kinds=(jnp.float32,), before=None):
+        given = rows if before is None else after(rows, before)
+        return project(blocks, splits, kinds, given, gate_weight, up_weight, slots, width)
 
     far, far_own = projected(
-        jnp.concatenate([theirs[1:], theirs[:1]]), (PLANE - 1, 1), (jnp.float32, jnp.bfloat16)
+        theirs[1:] + theirs[:1], (PLANE - 1, 1), (jnp.float32, jnp.bfloat16)
     )
     far, far_own = over_core(far), over_core(far_own)
     (chip,) = projected(mine[1:], (PLANE - 1,))
     chip = (chip + far).astype(jnp.bfloat16)
-    (kept,) = projected(after(mine[:1], chip), (1,))
+    (kept,) = projected(mine[:1], (1,), before=chip)
     halves = 2 if slots > 1 else 1
     top = me // (slivers // 2) if halves == 2 else 0
     length = slots // halves
@@ -296,12 +321,12 @@
         gathered.append([hidden] + [over_sliver(hidden, d) for d in range(1, PLANE)])
 
     (gathered,) = gathered
-    order = jnp.stack([mine[0], theirs[0]])
+    order = mine[:1] + theirs[:1]
     first = [gathered[0], over_core(gathered[0])]
     mixed = mix(order, routes_padded, first, down_weight, None, jnp.float32)
     rest = [after(x, mixed) for x in gathered[1:]]
     rest_other = [over_core(x) for x in rest]
-    order = jnp.concatenate([mine[1:], theirs[1:]])
+    order = mine[1:] + theirs[1:]
     mixed = mix(order, routes_padded, rest + rest_other, down_weight, mixed, jnp.bfloat16)
 
     pieces = mixed.reshape(devices, own_rows, depth)

time: 80.8 us -> 78.4 us (0.970)
  blocking collectives: 9.11 us -> 22.8 us
  starting transfers between devices: 20.7 us -> 13.2 us
  waiting for transfers between devices: 20.7 us -> 15.4 us
  Pallas kernels: 27.5 us -> 24.7 us
    all_to_all x0 -> x1, blocking collectives: none -> 13.7 us  [shards(): rows = lax.all_to_all(pieces, ('rep', 'sliver'), 0, 0, tiled=True)]
    all_to_all x1 -> x0, starting transfers between devices: 7.36 us -> none  [shards(): rows = lax.all_to_all(pieces, ('rep', 'sliver'), 0, 0, tiled=True)]
    all_to_all x1 -> x0, waiting for transfers between devices: 6.3 us -> none  [shards(): rows = lax.all_to_all(pieces, ('rep', 'sliver'), 0, 0, tiled=True)]
    pallas_call x6, Pallas kernels: 27.5 us -> 24.7 us  [the longest x3 14.7 us: project(): pl.pallas_call(functools.partial(project_kernel, blocks), out_shape=[jax....]
    ppermute x11, waiting for transfers between devices: 13.2 us -> 14.1 us  [over_sliver(): return lax.ppermute(x, 'sliver', [(i, i ^ d) for i in range(slivers)])]
  transfers between devices with their start and end apart: 18 -> 17, of which waited for: 9 -> 8; matrix products, arithmetic and copies ran while one was open for 2% -> 1% of each run, Pallas kernels for 15% -> 14%
where the time goes in v3:
time: 78.4 us; the launch traced here: 78.1 us
  Pallas kernels  24.7 us (32%)
  blocking collectives  22.8 us (29%)
  waiting for transfers between devices  15.4 us (20%)
  starting transfers between devices  13.2 us (17%)
  other arithmetic  0.99 us (1%)
  local copies, waits for them, and re-layouts  0.79 us (1%)
    pallas_call x3, Pallas kernels, project(): pl.pallas_call(functools.partial(project_kernel, blocks), out_shape=[jax....  14.7 us
    ppermute x11, waiting for transfers between devices, over_sliver(): return lax.ppermute(x, 'sliver', [(i, i ^ d) for i in range(slivers)])  14.1 us
    all_to_all x1, blocking collectives, shards(): rows = lax.all_to_all(pieces, ('rep', 'sliver'), 0, 0, tiled=True)  13.7 us
    ppermute x11, starting transfers between devices, over_sliver(): return lax.ppermute(x, 'sliver', [(i, i ^ d) for i in range(slivers)])  12.5 us
    pallas_call x2, Pallas kernels, mix(): pl.pallas_call(functools.partial(mix_kernel, blocks, extra is not None),...  9.25 us
    all_to_all x1, blocking collectives, shards(): pieces = lax.all_to_all(pieces, ('rep', 'sliver'), 0, 0, tiled=True)  9.11 us
  transfers between devices with their start and end apart: 17, of which 8 were waited for; matrix products, arithmetic and copies ran while one was open for 1% of the time, Pallas kernels for 14%

profile of v3, /device:TPU:0, one launch (start us, length us, event | category | flops | bytes accessed | tf_op | source)
XLA Modules:
  0.0 78.1 jit_solution(3428514038112489693)
XLA Ops:
  0.0 0.8 %shard_map.64 = bf16[16,2,384]{2,1,0:T(2,128)(2,1)S(1)} custom-call(bf16[2,4096]{1,0:T(2,128)(2,1)} %tokens_hbm.1, s32[2,2]{1,0:T(2,128)} %routes_hbm.1, s32[2,2]{1,0:T(2,128)} %scores_hbm.1), custom_call_target="tpu_custom_call" | custom-call | tf_op jit(solution)/shard_map/pallas_call | solution.py:59
  0.8 13.7 %all_to_all.10 = bf16[16,2,384]{2,1,0:T(2,128)(2,1)S(1)} all-to-all(bf16[16,2,384]{2,1,0:T(2,128)(2,1)S(1)} %shard_map.64), channel_id=1, replica_groups=mesh['group'=2,'sliver'=8,'rep'=2] {'rep','sliver'}, dimensions={0} | all-to-all | bytes 49152 | tf_op jit(solution)/shard_map/all_to_all | solution.py:249
  14.5 6.6 %shard_map.66 = (f32[3,2,2,32,1024]{4,3,2,1,0:T(8,128)S(1)}, bf16[1,2,2,32,1024]{4,3,2,1,0:T(8,128)(2,1)S(1)}) custom-call(bf16[32,384]{1,0:T(8,128)(2,1)S(1)} %reshape.135.rows_ref, bf16[256,32768]{1,0:T(8,128)(2,1)} %gate_ref.5, bf16[256,32768]{1,0:T(8,128)(2,1)} %up_ref.5), custom_call_target="tpu_custom_call" | custom-call | flops 1073741824 | bytes 16777216 | tf_op jit(solution)/shard_map/pallas_call | solution.py:134
  21.1 0.1 collective-permute-start
  21.3 0.5 collective-permute-start.4
  21.7 5.3 %shard_map.65 = f32[3,2,2,32,1024]{4,3,2,1,0:T(8,128)S(1)} custom-call(bf16[32,384]{1,0:T(8,128)(2,1)S(1)} %reshape.135.rows_ref, bf16[256,32768]{1,0:T(8,128)(2,1)} %gate_ref.5, bf16[256,32768]{1,0:T(8,128)(2,1)} %up_ref.5), custom_call_target="tpu_custom_call" | custom-call | flops 805306368 | bytes 12582912 | tf_op jit(solution)/shard_map/pallas_call | solution.py:134
  27.1 0.0 collective-permute-done
  27.1 0.3 add_convert_fusion
  27.4 0.1 fusion.6
  27.5 0.6 collective-permute-start.5
  28.2 0.6 collective-permute-start.6
  28.8 2.4 %collective-permute-start.7 = (bf16[1,2,32,1024]{3,2,1,0:T(8,128)(2,1)S(1)}, bf16[1,2,32,1024]{3,2,1,0:T(8,128)(2,1)S(1)}, u32[]{:S(2)}, u32[]{:S(2)}) collective-permute-start(bf16[1,2,32,1024]{3,2,1,0:T(8,128)(2,1)S(1)} %get-tuple-element.25), channel_id=1, source_target_pairs={{0,6},{2,4},{4,2},{6,0},{8,14},{10,12},{12,10},{14,8},{1,7},{3,5},... | collective-permute-start | bytes 393224 | tf_op jit(solution)/shard_map/ppermute | solution.py:246
  31.2 0.6 collective-permute-start.1
  31.8 2.7 %shard_map.67 = f32[1,2,2,32,1024]{4,3,2,1,0:T(8,128)S(1)} custom-call(bf16[32,384]{1,0:T(8,128)(2,1)S(1)} %reshape.135.rows_ref, bf16[256,32768]{1,0:T(8,128)(2,1)} %gate_ref.5, bf16[256,32768]{1,0:T(8,128)(2,1)} %up_ref.5), custom_call_target="tpu_custom_call" | custom-call | flops 268435456 | bytes 4194304 | tf_op jit(solution)/shard_map/pallas_call | solution.py:134
  34.5 0.0 collective-permute-done.4
  34.5 0.6 collective-permute-start.2
  35.2 0.0 collective-permute-done.5
  35.2 2.3 %collective-permute-start.3 = (bf16[1,2,32,1024]{3,2,1,0:T(8,128)(2,1)S(1)}, bf16[1,2,32,1024]{3,2,1,0:T(8,128)(2,1)S(1)}, u32[]{:S(2)}, u32[]{:S(2)}) collective-permute-start(bf16[1,2,32,1024]{3,2,1,0:T(8,128)(2,1)S(1)} %get-tuple-element.24), channel_id=1, source_target_pairs={{0,6},{2,4},{4,2},{6,0},{8,14},{10,12},{12,10},{14,8},{1,7},{3,5},... | collective-permute-start | bytes 393224 | tf_op jit(solution)/shard_map/ppermute | solution.py:246
  37.5 0.0 collective-permute-done.6
  37.5 0.0 collective-permute-done.7
  37.5 0.1 fusion
  37.6 0.7 collective-permute-start.8
  38.3 0.2 slice_reduce_fusion
  38.5 0.2 convert_reduce_fusion
  38.7 0.6 collective-permute-done.1
  39.3 2.3 %collective-permute-done.2 = bf16[1,2,32,1024]{3,2,1,0:T(8,128)(2,1)S(1)} collective-permute-done((bf16[1,2,32,1024]{3,2,1,0:T(8,128)(2,1)S(1)}, bf16[1,2,32,1024]{3,2,1,0:T(8,128)(2,1)S(1)}, u32[]{:S(2)}, u32[]{:S(2)}) %collective-permute-start.2) | collective-permute-done | bytes 131104 | tf_op jit(solution)/shard_map/ppermute | solution.py:246
  41.5 4.1 %collective-permute-done.3 = bf16[1,2,32,1024]{3,2,1,0:T(8,128)(2,1)S(1)} collective-permute-done((bf16[1,2,32,1024]{3,2,1,0:T(8,128)(2,1)S(1)}, bf16[1,2,32,1024]{3,2,1,0:T(8,128)(2,1)S(1)}, u32[]{:S(2)}, u32[]{:S(2)}) %collective-permute-start.3) | collective-permute-done | bytes 131104 | tf_op jit(solution)/shard_map/ppermute | solution.py:246
  45.6 0.0 collective-permute-done.8
  45.6 0.1 fusion.1
  45.7 0.1 fusion.4
  45.8 1.1 %collective-permute-start.9 = (bf16[1,32,1024]{2,1,0:T(8,128)(2,1)S(1)}, bf16[1,32,1024]{2,1,0:T(8,128)(2,1)S(1)}, u32[]{:S(2)}, u32[]{:S(2)}) collective-permute-start(bf16[1,32,1024]{2,1,0:T(8,128)(2,1)S(1)} %fusion.4), channel_id=1, source_target_pairs={{0,8},{2,10},{4,12},{6,14},{8,0},{10,2},{12,4},{14,6},{1,9},{3,11}... | collective-permute-start | bytes 196616 | tf_op jit(solution)/shard_map/ppermute | solution.py:246
  46.9 4.1 %collective-permute-done.9 = bf16[1,32,1024]{2,1,0:T(8,128)(2,1)S(1)} collective-permute-done((bf16[1,32,1024]{2,1,0:T(8,128)(2,1)S(1)}, bf16[1,32,1024]{2,1,0:T(8,128)(2,1)S(1)}, u32[]{:S(2)}, u32[]{:S(2)}) %collective-permute-start.9) | collective-permute-done | bytes 65568 | tf_op jit(solution)/shard_map/ppermute | solution.py:246
  51.1 0.1 collective-permute-start.11
  51.1 0.8 %collective-permute-start.13 = (bf16[64,1024]{1,0:T(8,128)(2,1)S(1)}, bf16[64,1024]{1,0:T(8,128)(2,1)S(1)}, u32[]{:S(2)}, u32[]{:S(2)}) collective-permute-start(bf16[64,1024]{1,0:T(8,128)(2,1)S(1)} %bitcast.44), channel_id=1, source_target_pairs={{0,6},{2,4},{4,2},{6,0},{8,14},{10,12},{12,10},{14,8},{1,7},{3,5},... | collective-permute-start | bytes 393224 | tf_op jit(solution)/shard_map/ppermute | solution.py:246
  52.0 0.8 collective-permute-start.12
  52.7 2.0 %collective-permute-start.10 = (bf16[64,1024]{1,0:T(8,128)(2,1)S(1)}, bf16[64,1024]{1,0:T(8,128)(2,1)S(1)}, u32[]{:S(2)}, u32[]{:S(2)}) collective-permute-start(bf16[64,1024]{1,0:T(8,128)(2,1)S(1)} %bitcast.46), channel_id=1, source_target_pairs={{0,2},{2,0},{4,6},{6,4},{8,10},{10,8},{12,14},{14,12},{1,3},{3,1},... | collective-permute-start | bytes 393224 | tf_op jit(solution)/shard_map/ppermute | solution.py:246
  54.7 0.0 collective-permute-done.11.refs_1_
  54.7 3.1 %shard_map.68.refs_7_ = f32[32,256]{1,0:T(8,128)S(1)} custom-call(f32[32,128]{1,0:T(8,128)S(1)} %pad.4.routes_ref, bf16[64,1024]{1,0:T(8,128)(2,1)S(1)} %bitcast.47, bf16[64,1024]{1,0:T(8,128)(2,1)S(1)} %collective-permute-done.11.refs_1_, bf16[256,32768]{1,0:T(8,128)(2,1)} %refs_6_.1), custom_call_target="tpu_custom_call" | custom-call | flops 134217728 | bytes 4194304 | tf_op jit(solution)/shard_map/pallas_call | solution.py:214
  57.8 0.7 collective-permute-done.13.refs_2_
  58.4 0.0 collective-permute-start.16
  58.4 0.9 %collective-permute-done.12.refs_1_ = bf16[64,1024]{1,0:T(8,128)(2,1)S(1)} collective-permute-done((bf16[64,1024]{1,0:T(8,128)(2,1)S(1)}, bf16[64,1024]{1,0:T(8,128)(2,1)S(1)}, u32[]{:S(2)}, u32[]{:S(2)}) %collective-permute-start.12) | collective-permute-done | bytes 131104 | tf_op jit(solution)/shard_map/ppermute | solution.py:246
  59.4 0.0 collective-permute-start.15
  59.4 1.4 %collective-permute-done.10.refs_0_ = bf16[64,1024]{1,0:T(8,128)(2,1)S(1)} collective-permute-done((bf16[64,1024]{1,0:T(8,128)(2,1)S(1)}, bf16[64,1024]{1,0:T(8,128)(2,1)S(1)}, u32[]{:S(2)}, u32[]{:S(2)}) %collective-permute-start.10) | collective-permute-done | bytes 131104 | tf_op jit(solution)/shard_map/ppermute | solution.py:246
  60.8 0.0 collective-permute-start.14
  60.8 0.0 collective-permute-done.16.refs_5_
  60.8 0.0 collective-permute-done.15.refs_4_
  60.8 1.3 %collective-permute-done.14.refs_3_ = bf16[64,1024]{1,0:T(8,128)(2,1)S(1)} collective-permute-done((bf16[64,1024]{1,0:T(8,128)(2,1)S(1)}, bf16[64,1024]{1,0:T(8,128)(2,1)S(1)}, u32[]{:S(2)}, u32[]{:S(2)}) %collective-permute-start.14) | collective-permute-done | bytes 131104 | tf_op jit(solution)/shard_map/ppermute | solution.py:243
  62.1 6.2 %shard_map.69 = bf16[32,256]{1,0:T(8,128)(2,1)S(1)} custom-call(f32[32,128]{1,0:T(8,128)S(1)} %pad.4.routes_ref, bf16[64,1024]{1,0:T(8,128)(2,1)S(1)} %collective-permute-done.10.refs_0_, bf16[64,1024]{1,0:T(8,128)(2,1)S(1)} %collective-permute-done.12.refs_1_, bf16[64,1024]{1,0:T(8,128)(2,1)S(1)} %collective-permute-done.13.refs_2_, ...), custom_call_target="tpu_custom_call" | custom-call | flops 402653184 | bytes 12582912 | tf_op jit(solution)/shard_map/pallas_call | solution.py:214
  68.3 9.1 %all_to_all.11 = bf16[16,2,256]{2,1,0:T(2,128)(2,1)S(1)} all-to-all(bf16[16,2,256]{2,1,0:T(2,128)(2,1)S(1)} %reshape.136), channel_id=1, replica_groups=mesh['group'=2,'sliver'=8,'rep'=2] {'rep','sliver'}, dimensions={0} | all-to-all | bytes 32768 | tf_op jit(solution)/shard_map/all_to_all | solution.py:333
  77.4 0.6 reshape.138
  (9 shorter events, 0.1 us)
Async XLA Ops:
  21.1 5.9 %collective-permute-start = (f32[3,2,2,32,1024]{4,3,2,1,0:T(8,128)S(1)}, f32[3,2,2,32,1024]{4,3,2,1,0:T(8,128)S(1)}, u32[]{:S(2)}, u32[]{:S(2)}) collective-permute-start(f32[3,2,2,32,1024]{4,3,2,1,0:T(8,128)S(1)} %get-tuple-element.11), channel_id=1, source_target_pairs={{0,1},{1,0},{2,3},{3,2},{4,5},{5,4},{6,7},{7,6},{8,9},{9,8},{10,11... | collective-permute-start | bytes 4718600 | tf_op jit(solution)/shard_map/ppermute | solution.py:243
  21.3 13.3 %collective-permute-start.4 = (bf16[1,2,2,32,1024]{4,3,2,1,0:T(8,128)(2,1)S(1)}, bf16[1,2,2,32,1024]{4,3,2,1,0:T(8,128)(2,1)S(1)}, u32[]{:S(2)}, u32[]{:S(2)}) collective-permute-start(bf16[1,2,2,32,1024]{4,3,2,1,0:T(8,128)(2,1)S(1)} %get-tuple-element.13), channel_id=1, source_target_pairs={{0,1},{1,0},{2,3},{3,2},{4,5},{5,4},{6,7},{7,6},{8,9},{9,8},{10,11... | collective-permute-start | bytes 786440 | tf_op jit(solution)/shard_map/ppermute | solution.py:243
  27.5 7.7 %collective-permute-start.5 = (bf16[1,2,32,1024]{3,2,1,0:T(8,128)(2,1)S(1)}, bf16[1,2,32,1024]{3,2,1,0:T(8,128)(2,1)S(1)}, u32[]{:S(2)}, u32[]{:S(2)}) collective-permute-start(bf16[1,2,32,1024]{3,2,1,0:T(8,128)(2,1)S(1)} %get-tuple-element.21), channel_id=1, source_target_pairs={{0,2},{2,0},{4,6},{6,4},{8,10},{10,8},{12,14},{14,12},{1,3},{3,1},... | collective-permute-start | bytes 393224 | tf_op jit(solution)/shard_map/ppermute | solution.py:246
  28.2 9.4 %collective-permute-start.6 = (bf16[1,2,32,1024]{3,2,1,0:T(8,128)(2,1)S(1)}, bf16[1,2,32,1024]{3,2,1,0:T(8,128)(2,1)S(1)}, u32[]{:S(2)}, u32[]{:S(2)}) collective-permute-start(bf16[1,2,32,1024]{3,2,1,0:T(8,128)(2,1)S(1)} %get-tuple-element.23), channel_id=1, source_target_pairs={{0,4},{2,6},{4,0},{6,2},{8,12},{10,14},{12,8},{14,10},{1,5},{3,7},... | collective-permute-start | bytes 393224 | tf_op jit(solution)/shard_map/ppermute | solution.py:246
  28.8 8.7 %collective-permute-start.7 = (bf16[1,2,32,1024]{3,2,1,0:T(8,128)(2,1)S(1)}, bf16[1,2,32,1024]{3,2,1,0:T(8,128)(2,1)S(1)}, u32[]{:S(2)}, u32[]{:S(2)}) collective-permute-start(bf16[1,2,32,1024]{3,2,1,0:T(8,128)(2,1)S(1)} %get-tuple-element.25), channel_id=1, source_target_pairs={{0,6},{2,4},{4,2},{6,0},{8,14},{10,12},{12,10},{14,8},{1,7},{3,5},... | collective-permute-start | bytes 393224 | tf_op jit(solution)/shard_map/ppermute | solution.py:246
  31.2 8.1 %collective-permute-start.1 = (bf16[1,2,32,1024]{3,2,1,0:T(8,128)(2,1)S(1)}, bf16[1,2,32,1024]{3,2,1,0:T(8,128)(2,1)S(1)}, u32[]{:S(2)}, u32[]{:S(2)}) collective-permute-start(bf16[1,2,32,1024]{3,2,1,0:T(8,128)(2,1)S(1)} %get-tuple-element.20), channel_id=1, source_target_pairs={{0,2},{2,0},{4,6},{6,4},{8,10},{10,8},{12,14},{14,12},{1,3},{3,1},... | collective-permute-start | bytes 393224 | tf_op jit(solution)/shard_map/ppermute | solution.py:246
  34.5 7.0 %collective-permute-start.2 = (bf16[1,2,32,1024]{3,2,1,0:T(8,128)(2,1)S(1)}, bf16[1,2,32,1024]{3,2,1,0:T(8,128)(2,1)S(1)}, u32[]{:S(2)}, u32[]{:S(2)}) collective-permute-start(bf16[1,2,32,1024]{3,2,1,0:T(8,128)(2,1)S(1)} %get-tuple-element.22), channel_id=1, source_target_pairs={{0,4},{2,6},{4,0},{6,2},{8,12},{10,14},{12,8},{14,10},{1,5},{3,7},... | collective-permute-start | bytes 393224 | tf_op jit(solution)/shard_map/ppermute | solution.py:246
  35.2 10.4 %collective-permute-start.3 = (bf16[1,2,32,1024]{3,2,1,0:T(8,128)(2,1)S(1)}, bf16[1,2,32,1024]{3,2,1,0:T(8,128)(2,1)S(1)}, u32[]{:S(2)}, u32[]{:S(2)}) collective-permute-start(bf16[1,2,32,1024]{3,2,1,0:T(8,128)(2,1)S(1)} %get-tuple-element.24), channel_id=1, source_target_pairs={{0,6},{2,4},{4,2},{6,0},{8,14},{10,12},{12,10},{14,8},{1,7},{3,5},... | collective-permute-start | bytes 393224 | tf_op jit(solution)/shard_map/ppermute | solution.py:246
  37.6 8.0 %collective-permute-start.8 = (bf16[1,2,32,1024]{3,2,1,0:T(8,128)(2,1)S(1)}, bf16[1,2,32,1024]{3,2,1,0:T(8,128)(2,1)S(1)}, u32[]{:S(2)}, u32[]{:S(2)}) collective-permute-start(bf16[1,2,32,1024]{3,2,1,0:T(8,128)(2,1)S(1)} %fusion), channel_id=1, source_target_pairs={{0,8},{2,10},{4,12},{6,14},{8,0},{10,2},{12,4},{14,6},{1,9},{3,11}... | collective-permute-start | bytes 393224 | tf_op jit(solution)/shard_map/ppermute | solution.py:246
  45.8 5.2 %collective-permute-start.9 = (bf16[1,32,1024]{2,1,0:T(8,128)(2,1)S(1)}, bf16[1,32,1024]{2,1,0:T(8,128)(2,1)S(1)}, u32[]{:S(2)}, u32[]{:S(2)}) collective-permute-start(bf16[1,32,1024]{2,1,0:T(8,128)(2,1)S(1)} %fusion.4), channel_id=1, source_target_pairs={{0,8},{2,10},{4,12},{6,14},{8,0},{10,2},{12,4},{14,6},{1,9},{3,11}... | collective-permute-start | bytes 196616 | tf_op jit(solution)/shard_map/ppermute | solution.py:246
  51.1 3.6 %collective-permute-start.11 = (bf16[64,1024]{1,0:T(8,128)(2,1)S(1)}, bf16[64,1024]{1,0:T(8,128)(2,1)S(1)}, u32[]{:S(2)}, u32[]{:S(2)}) collective-permute-start(bf16[64,1024]{1,0:T(8,128)(2,1)S(1)} %bitcast.43), channel_id=1, source_target_pairs={{0,1},{1,0},{2,3},{3,2},{4,5},{5,4},{6,7},{7,6},{8,9},{9,8},{10,11... | collective-permute-start | bytes 393224 | tf_op jit(solution)/shard_map/ppermute | solution.py:243
  51.1 7.3 %collective-permute-start.13 = (bf16[64,1024]{1,0:T(8,128)(2,1)S(1)}, bf16[64,1024]{1,0:T(8,128)(2,1)S(1)}, u32[]{:S(2)}, u32[]{:S(2)}) collective-permute-start(bf16[64,1024]{1,0:T(8,128)(2,1)S(1)} %bitcast.44), channel_id=1, source_target_pairs={{0,6},{2,4},{4,2},{6,0},{8,14},{10,12},{12,10},{14,8},{1,7},{3,5},... | collective-permute-start | bytes 393224 | tf_op jit(solution)/shard_map/ppermute | solution.py:246
  52.0 7.4 %collective-permute-start.12 = (bf16[64,1024]{1,0:T(8,128)(2,1)S(1)}, bf16[64,1024]{1,0:T(8,128)(2,1)S(1)}, u32[]{:S(2)}, u32[]{:S(2)}) collective-permute-start(bf16[64,1024]{1,0:T(8,128)(2,1)S(1)} %bitcast.45), channel_id=1, source_target_pairs={{0,4},{2,6},{4,0},{6,2},{8,12},{10,14},{12,8},{14,10},{1,5},{3,7},... | collective-permute-start | bytes 393224 | tf_op jit(solution)/shard_map/ppermute | solution.py:246
  52.7 8.0 %collective-permute-start.10 = (bf16[64,1024]{1,0:T(8,128)(2,1)S(1)}, bf16[64,1024]{1,0:T(8,128)(2,1)S(1)}, u32[]{:S(2)}, u32[]{:S(2)}) collective-permute-start(bf16[64,1024]{1,0:T(8,128)(2,1)S(1)} %bitcast.46), channel_id=1, source_target_pairs={{0,2},{2,0},{4,6},{6,4},{8,10},{10,8},{12,14},{14,12},{1,3},{3,1},... | collective-permute-start | bytes 393224 | tf_op jit(solution)/shard_map/ppermute | solution.py:246
  58.4 2.4 %collective-permute-start.16 = (bf16[64,1024]{1,0:T(8,128)(2,1)S(1)}, bf16[64,1024]{1,0:T(8,128)(2,1)S(1)}, u32[]{:S(2)}, u32[]{:S(2)}) collective-permute-start(bf16[64,1024]{1,0:T(8,128)(2,1)S(1)} %collective-permute-done.13.refs_2_), channel_id=1, source_target_pairs={{0,1},{1,0},{2,3},{3,2},{4,5},{5,4},{6,7},{7,6},{8,9},{9,8},{10,11... | collective-permute-start | bytes 393224 | tf_op jit(solution)/shard_map/ppermute | solution.py:243
  59.4 1.4 %collective-permute-start.15 = (bf16[64,1024]{1,0:T(8,128)(2,1)S(1)}, bf16[64,1024]{1,0:T(8,128)(2,1)S(1)}, u32[]{:S(2)}, u32[]{:S(2)}) collective-permute-start(bf16[64,1024]{1,0:T(8,128)(2,1)S(1)} %collective-permute-done.12.refs_1_), channel_id=1, source_target_pairs={{0,1},{1,0},{2,3},{3,2},{4,5},{5,4},{6,7},{7,6},{8,9},{9,8},{10,11... | collective-permute-start | bytes 393224 | tf_op jit(solution)/shard_map/ppermute | solution.py:243
  60.8 1.3 %collective-permute-start.14 = (bf16[64,1024]{1,0:T(8,128)(2,1)S(1)}, bf16[64,1024]{1,0:T(8,128)(2,1)S(1)}, u32[]{:S(2)}, u32[]{:S(2)}) collective-permute-start(bf16[64,1024]{1,0:T(8,128)(2,1)S(1)} %collective-permute-done.10.refs_0_), channel_id=1, source_target_pairs={{0,1},{1,0},{2,3},{3,2},{4,5},{5,4},{6,7},{7,6},{8,9},{9,8},{10,11... | collective-permute-start | bytes 393224 | tf_op jit(solution)/shard_map/ppermute | solution.py:243

commit v4 on v3

--- a/solution.py
+++ b/solution.py
@@ -148,13 +148,13 @@
     )(rows, in_hbm(gate_weight), in_hbm(up_weight))
 
 
-def mix_kernel(blocks, added, routes_ref, *refs):
+def mix_kernel(blocks, added, cores, routes_ref, *refs):
     steps = len(blocks)
     hidden, refs = refs[:steps], refs[steps:]
     down_ref, refs = refs[0], refs[1:]
     extra = refs[0] if added else None
     out_ref, stacked, buffer, sems = refs[-4:]
-    count, depth = out_ref.shape
+    count, depth = routes_ref.shape[0], out_ref.shape[-1]
     cols = hidden[0].shape[1]
     per_expert = down_ref.shape[1] // (EXPERTS * cols)
     copies = []
@@ -192,19 +192,26 @@
         return total
 
     total = extra[...] if added else jnp.zeros((count, depth), jnp.float32)
-    total = lax.fori_loop(0, steps, step, total)
-    out_ref[...] = total.astype(out_ref.dtype)
-
-
-def mix(blocks, routes, hidden, down_weight, extra, kind):
+    total = lax.fori_loop(0, steps, step, total).astype(out_ref.dtype)
+    if not cores:
+        out_ref[...] = total
+    else:
+        devices, own_rows, _ = out_ref.shape
+        for place in range(devices):
+            first = (place % cores * (devices // cores) + place // cores) * own_rows
+            out_ref[place] = total[first : first + own_rows]
+
+
+def mix(blocks, routes, hidden, down_weight, extra, kind, shape, cores):
     count, depth = routes.shape[0], down_weight.shape[0]
     width = hidden[0].shape[1]
     steps = len(hidden)
     room = 16 * steps * count * width
     if room > 32 * MIB and steps > 1:
         part = steps // 2
-        extra = mix(blocks[:part], routes, hidden[:part], down_weight, extra, jnp.float32)
-        return mix(blocks[part:], routes, hidden[part:], down_weight, extra, kind)
+        some, whole = blocks[:part], (count, depth)
+        extra = mix(some, routes, hidden[:part], down_weight, extra, jnp.float32, whole, 0)
+        return mix(blocks[part:], routes, hidden[part:], down_weight, extra, kind, shape, cores)
     weights = steps * EXPERTS * depth * width
     operands = [routes, *hidden, in_hbm(down_weight)]
     specs = [VMEM] * (1 + steps) + [ANY]
@@ -212,8 +219,8 @@
         operands.append(extra)
         specs.append(VMEM)
     return pl.pallas_call(
-        functools.partial(mix_kernel, blocks, extra is not None),
-        out_shape=jax.ShapeDtypeStruct((count, depth), kind),
+        functools.partial(mix_kernel, blocks, extra is not None, cores),
+        out_shape=jax.ShapeDtypeStruct(shape, kind),
         in_specs=specs,
         out_specs=VMEM,
         scratch_shapes=[
@@ -323,16 +330,19 @@
     (gathered,) = gathered
     order = mine[:1] + theirs[:1]
     first = [gathered[0], over_core(gathered[0])]
-    mixed = mix(order, routes_padded, first, down_weight, None, jnp.float32)
-    rest = [after(x, mixed) for x in gathered[1:]]
-    rest_other = [over_core(x) for x in rest]
-    order = mine[1:] + theirs[1:]
-    mixed = mix(order, routes_padded, rest + rest_other, down_weight, mixed, jnp.bfloat16)
-
-    pieces = mixed.reshape(devices, own_rows, depth)
-    pieces = lax.all_to_all(pieces, ("rep", "sliver"), 0, 0, tiled=True)
-    pieces = pieces.reshape(cores, slivers, own_rows, depth)
-    return jnp.transpose(pieces, (2, 1, 0, 3)).reshape(own_rows, model)
+    shape = (count, depth)
+    mixed = mix(order, routes_padded, first, down_weight, None, jnp.float32, shape, 0)
+    last = PLANE - 1
+    early = after(gathered[last], mixed)
+    early_other = over_core(early)
+    mixed = mix(mine[last:], routes_padded, [early], down_weight, mixed, jnp.float32, shape, 0)
+    rest = [after(x, mixed) for x in gathered[1:last]]
+    rest += [over_core(x) for x in rest] + [early_other]
+    order = mine[1:last] + theirs[1:]
+    shape = (devices, own_rows, depth)
+    pieces = mix(order, routes_padded, rest, down_weight, mixed, jnp.bfloat16, shape, cores)
+    pieces = lax.all_to_all(pieces, ("sliver", "rep"), 0, 0, tiled=True)
+    return jnp.transpose(pieces, (1, 0, 2)).reshape(own_rows, model)
 
 
 def solution(mesh):

time: 78.4 us -> 78.1 us (level)
  waiting for transfers between devices: 15.4 us -> 13 us
  Pallas kernels: 24.7 us -> 26.3 us
    ppermute x11, waiting for transfers between devices: 14.1 us -> 11.8 us  [over_sliver(): return lax.ppermute(x, 'sliver', [(i, i ^ d) for i in range(slivers)])]
    pallas_call x2 -> x3, Pallas kernels: 9.25 us -> 10.8 us  [mix(): pl.pallas_call(functools.partial(mix_kernel, blocks, extra is not None, c...]
  transfers between devices with their start and end apart: 17 -> 17, of which waited for: 8 -> 8; matrix products, arithmetic and copies ran while one was open for 1% -> 1% of each run, Pallas kernels for 14% -> 17%
where the time goes in v4:
time: 78.1 us; the launch traced here: 77.8 us
  Pallas kernels  26.3 us (34%)
  blocking collectives  22.8 us (29%)
  starting transfers between devices  13.8 us (18%)
  waiting for transfers between devices  13 us (17%)
  other arithmetic  0.99 us (1%)
    pallas_call x3, Pallas kernels, project(): pl.pallas_call(functools.partial(project_kernel, blocks), out_shape=[jax....  14.7 us
    all_to_all x1, blocking collectives, shards(): rows = lax.all_to_all(pieces, ('rep', 'sliver'), 0, 0, tiled=True)  13.7 us
    ppermute x11, starting transfers between devices, over_sliver(): return lax.ppermute(x, 'sliver', [(i, i ^ d) for i in range(slivers)])  12.5 us
    ppermute x11, waiting for transfers between devices, over_sliver(): return lax.ppermute(x, 'sliver', [(i, i ^ d) for i in range(slivers)])  11.8 us
    pallas_call x3, Pallas kernels, mix(): pl.pallas_call(functools.partial(mix_kernel, blocks, extra is not None, c...  10.8 us
    all_to_all x1, blocking collectives, shards(): pieces = lax.all_to_all(pieces, ('sliver', 'rep'), 0, 0, tiled=True)  9.11 us
  transfers between devices with their start and end apart: 17, of which 8 were waited for; matrix products, arithmetic and copies ran while one was open for 1% of the time, Pallas kernels for 17%

profile of v4, /device:TPU:0, one launch (start us, length us, event | category | flops | bytes accessed | tf_op | source)
XLA Modules:
  0.0 77.8 jit_solution(17779813164853610867)
XLA Ops:
  0.0 0.8 %shard_map.64 = bf16[16,2,384]{2,1,0:T(2,128)(2,1)S(1)} custom-call(bf16[2,4096]{1,0:T(2,128)(2,1)} %tokens_hbm.1, s32[2,2]{1,0:T(2,128)} %routes_hbm.1, s32[2,2]{1,0:T(2,128)} %scores_hbm.1), custom_call_target="tpu_custom_call" | custom-call | tf_op jit(solution)/shard_map/pallas_call | solution.py:59
  0.8 13.7 %all_to_all.10 = bf16[16,2,384]{2,1,0:T(2,128)(2,1)S(1)} all-to-all(bf16[16,2,384]{2,1,0:T(2,128)(2,1)S(1)} %shard_map.64), channel_id=1, replica_groups=mesh['group'=2,'sliver'=8,'rep'=2] {'rep','sliver'}, dimensions={0} | all-to-all | bytes 49152 | tf_op jit(solution)/shard_map/all_to_all | solution.py:256
  14.5 6.6 %shard_map.66 = (f32[3,2,2,32,1024]{4,3,2,1,0:T(8,128)S(1)}, bf16[1,2,2,32,1024]{4,3,2,1,0:T(8,128)(2,1)S(1)}) custom-call(bf16[32,384]{1,0:T(8,128)(2,1)S(1)} %reshape.129.rows_ref, bf16[256,32768]{1,0:T(8,128)(2,1)} %gate_ref.5, bf16[256,32768]{1,0:T(8,128)(2,1)} %up_ref.5), custom_call_target="tpu_custom_call" | custom-call | flops 1073741824 | bytes 16777216 | tf_op jit(solution)/shard_map/pallas_call | solution.py:134
  21.1 0.1 collective-permute-start
  21.3 0.5 collective-permute-start.4
  21.7 5.3 %shard_map.65 = f32[3,2,2,32,1024]{4,3,2,1,0:T(8,128)S(1)} custom-call(bf16[32,384]{1,0:T(8,128)(2,1)S(1)} %reshape.129.rows_ref, bf16[256,32768]{1,0:T(8,128)(2,1)} %gate_ref.5, bf16[256,32768]{1,0:T(8,128)(2,1)} %up_ref.5), custom_call_target="tpu_custom_call" | custom-call | flops 805306368 | bytes 12582912 | tf_op jit(solution)/shard_map/pallas_call | solution.py:134
  27.1 0.0 collective-permute-done
  27.1 0.3 add_convert_fusion
  27.4 0.1 fusion.6
  27.5 0.6 collective-permute-start.5
  28.2 0.6 collective-permute-start.6
  28.8 2.4 %collective-permute-start.7 = (bf16[1,2,32,1024]{3,2,1,0:T(8,128)(2,1)S(1)}, bf16[1,2,32,1024]{3,2,1,0:T(8,128)(2,1)S(1)}, u32[]{:S(2)}, u32[]{:S(2)}) collective-permute-start(bf16[1,2,32,1024]{3,2,1,0:T(8,128)(2,1)S(1)} %get-tuple-element.25), channel_id=1, source_target_pairs={{0,6},{2,4},{4,2},{6,0},{8,14},{10,12},{12,10},{14,8},{1,7},{3,5},... | collective-permute-start | bytes 393224 | tf_op jit(solution)/shard_map/ppermute | solution.py:253
  31.2 0.6 collective-permute-start.1
  31.8 2.7 %shard_map.67 = f32[1,2,2,32,1024]{4,3,2,1,0:T(8,128)S(1)} custom-call(bf16[32,384]{1,0:T(8,128)(2,1)S(1)} %reshape.129.rows_ref, bf16[256,32768]{1,0:T(8,128)(2,1)} %gate_ref.5, bf16[256,32768]{1,0:T(8,128)(2,1)} %up_ref.5), custom_call_target="tpu_custom_call" | custom-call | flops 268435456 | bytes 4194304 | tf_op jit(solution)/shard_map/pallas_call | solution.py:134
  34.5 0.0 collective-permute-done.4
  34.5 0.6 collective-permute-start.2
  35.2 0.0 collective-permute-done.5
  35.2 2.3 %collective-permute-start.3 = (bf16[1,2,32,1024]{3,2,1,0:T(8,128)(2,1)S(1)}, bf16[1,2,32,1024]{3,2,1,0:T(8,128)(2,1)S(1)}, u32[]{:S(2)}, u32[]{:S(2)}) collective-permute-start(bf16[1,2,32,1024]{3,2,1,0:T(8,128)(2,1)S(1)} %get-tuple-element.24), channel_id=1, source_target_pairs={{0,6},{2,4},{4,2},{6,0},{8,14},{10,12},{12,10},{14,8},{1,7},{3,5},... | collective-permute-start | bytes 393224 | tf_op jit(solution)/shard_map/ppermute | solution.py:253
  37.5 0.0 collective-permute-done.6
  37.5 0.0 collective-permute-done.7
  37.5 0.1 fusion
  37.6 0.7 collective-permute-start.8
  38.3 0.2 slice_reduce_fusion
  38.5 0.2 convert_reduce_fusion
  38.7 0.6 collective-permute-done.1
  39.3 2.3 %collective-permute-done.2 = bf16[1,2,32,1024]{3,2,1,0:T(8,128)(2,1)S(1)} collective-permute-done((bf16[1,2,32,1024]{3,2,1,0:T(8,128)(2,1)S(1)}, bf16[1,2,32,1024]{3,2,1,0:T(8,128)(2,1)S(1)}, u32[]{:S(2)}, u32[]{:S(2)}) %collective-permute-start.2) | collective-permute-done | bytes 131104 | tf_op jit(solution)/shard_map/ppermute | solution.py:253
  41.5 4.1 %collective-permute-done.3 = bf16[1,2,32,1024]{3,2,1,0:T(8,128)(2,1)S(1)} collective-permute-done((bf16[1,2,32,1024]{3,2,1,0:T(8,128)(2,1)S(1)}, bf16[1,2,32,1024]{3,2,1,0:T(8,128)(2,1)S(1)}, u32[]{:S(2)}, u32[]{:S(2)}) %collective-permute-start.3) | collective-permute-done | bytes 131104 | tf_op jit(solution)/shard_map/ppermute | solution.py:253
  45.6 0.0 collective-permute-done.8
  45.6 0.1 fusion.1
  45.7 0.1 fusion.4
  45.8 1.1 %collective-permute-start.9 = (bf16[1,32,1024]{2,1,0:T(8,128)(2,1)S(1)}, bf16[1,32,1024]{2,1,0:T(8,128)(2,1)S(1)}, u32[]{:S(2)}, u32[]{:S(2)}) collective-permute-start(bf16[1,32,1024]{2,1,0:T(8,128)(2,1)S(1)} %fusion.4), channel_id=1, source_target_pairs={{0,8},{2,10},{4,12},{6,14},{8,0},{10,2},{12,4},{14,6},{1,9},{3,11}... | collective-permute-start | bytes 196616 | tf_op jit(solution)/shard_map/ppermute | solution.py:253
  46.9 4.1 %collective-permute-done.9 = bf16[1,32,1024]{2,1,0:T(8,128)(2,1)S(1)} collective-permute-done((bf16[1,32,1024]{2,1,0:T(8,128)(2,1)S(1)}, bf16[1,32,1024]{2,1,0:T(8,128)(2,1)S(1)}, u32[]{:S(2)}, u32[]{:S(2)}) %collective-permute-start.9) | collective-permute-done | bytes 65568 | tf_op jit(solution)/shard_map/ppermute | solution.py:253
  51.1 0.1 collective-permute-start.12
  51.1 0.8 %collective-permute-start.11 = (bf16[64,1024]{1,0:T(8,128)(2,1)S(1)}, bf16[64,1024]{1,0:T(8,128)(2,1)S(1)}, u32[]{:S(2)}, u32[]{:S(2)}) collective-permute-start(bf16[64,1024]{1,0:T(8,128)(2,1)S(1)} %bitcast.43), channel_id=1, source_target_pairs={{0,6},{2,4},{4,2},{6,0},{8,14},{10,12},{12,10},{14,8},{1,7},{3,5},... | collective-permute-start | bytes 393224 | tf_op jit(solution)/shard_map/ppermute | solution.py:253
  52.0 0.8 collective-permute-start.13
  52.7 2.0 %collective-permute-start.10 = (bf16[64,1024]{1,0:T(8,128)(2,1)S(1)}, bf16[64,1024]{1,0:T(8,128)(2,1)S(1)}, u32[]{:S(2)}, u32[]{:S(2)}) collective-permute-start(bf16[64,1024]{1,0:T(8,128)(2,1)S(1)} %bitcast.45), channel_id=1, source_target_pairs={{0,2},{2,0},{4,6},{6,4},{8,10},{10,8},{12,14},{14,12},{1,3},{3,1},... | collective-permute-start | bytes 393224 | tf_op jit(solution)/shard_map/ppermute | solution.py:253
  54.7 0.0 collective-permute-done.12.refs_1_
  54.7 3.1 %shard_map.68.refs_2_ = f32[32,256]{1,0:T(8,128)S(1)} custom-call(f32[32,128]{1,0:T(8,128)S(1)} %pad.4.routes_ref, bf16[64,1024]{1,0:T(8,128)(2,1)S(1)} %bitcast.46, bf16[64,1024]{1,0:T(8,128)(2,1)S(1)} %collective-permute-done.12.refs_1_, bf16[256,32768]{1,0:T(8,128)(2,1)} %refs_5_.1), custom_call_target="tpu_custom_call" | custom-call | flops 134217728 | bytes 4194304 | tf_op jit(solution)/shard_map/pallas_call | solution.py:221
  57.8 0.7 collective-permute-done.11.refs_0_
  58.4 2.3 %shard_map.69.refs_6_ = f32[32,256]{1,0:T(8,128)S(1)} custom-call(f32[32,128]{1,0:T(8,128)S(1)} %pad.4.routes_ref, bf16[64,1024]{1,0:T(8,128)(2,1)S(1)} %collective-permute-done.11.refs_0_, bf16[256,32768]{1,0:T(8,128)(2,1)} %refs_5_.1, f32[32,256]{1,0:T(8,128)S(1)} %shard_map.68.refs_2_), custom_call_target="tpu_custom_call" | custom-call | flops 67108864 | bytes 2097152 | tf_op jit(solution)/shard_map/pallas_call | solution.py:221
  60.8 0.0 collective-permute-done.13.refs_1_
  60.8 0.1 collective-permute-start.15
  60.8 0.0 collective-permute-done.10.refs_0_
  60.9 0.5 collective-permute-start.14
  61.3 0.1 collective-permute-start.16
  61.4 0.7 collective-permute-done.15.refs_3_
  62.2 0.2 collective-permute-done.14.refs_2_
  62.4 0.3 collective-permute-done.16.refs_4_
  62.7 5.4 %shard_map.70 = bf16[16,2,256]{2,1,0:T(2,128)(2,1)S(1)} custom-call(f32[32,128]{1,0:T(8,128)S(1)} %pad.4.routes_ref, bf16[64,1024]{1,0:T(8,128)(2,1)S(1)} %collective-permute-done.10.refs_0_, bf16[64,1024]{1,0:T(8,128)(2,1)S(1)} %collective-permute-done.13.refs_1_, bf16[64,1024]{1,0:T(8,128)(2,1)S(1)} %collective-permute-done.14.refs_2_, ...), custom_call_target="tpu_custom_call" | custom-call | flops 335544320 | bytes 10485760 | tf_op jit(solution)/shard_map/pallas_call | solution.py:221
  68.1 9.1 %all_to_all.11 = bf16[16,2,256]{2,1,0:T(2,128)(2,1)S(1)} all-to-all(bf16[16,2,256]{2,1,0:T(2,128)(2,1)S(1)} %shard_map.70), channel_id=1, replica_groups=mesh['group'=2,'sliver'=8,'rep'=2] {'sliver','rep'}, dimensions={0} | all-to-all | bytes 32768 | tf_op jit(solution)/shard_map/all_to_all | solution.py:344
  77.2 0.6 copy.8
  (7 shorter events, 0.1 us)
Async XLA Ops:
  21.1 5.9 %collective-permute-start = (f32[3,2,2,32,1024]{4,3,2,1,0:T(8,128)S(1)}, f32[3,2,2,32,1024]{4,3,2,1,0:T(8,128)S(1)}, u32[]{:S(2)}, u32[]{:S(2)}) collective-permute-start(f32[3,2,2,32,1024]{4,3,2,1,0:T(8,128)S(1)} %get-tuple-element.11), channel_id=1, source_target_pairs={{0,1},{1,0},{2,3},{3,2},{4,5},{5,4},{6,7},{7,6},{8,9},{9,8},{10,11... | collective-permute-start | bytes 4718600 | tf_op jit(solution)/shard_map/ppermute | solution.py:250
  21.3 13.3 %collective-permute-start.4 = (bf16[1,2,2,32,1024]{4,3,2,1,0:T(8,128)(2,1)S(1)}, bf16[1,2,2,32,1024]{4,3,2,1,0:T(8,128)(2,1)S(1)}, u32[]{:S(2)}, u32[]{:S(2)}) collective-permute-start(bf16[1,2,2,32,1024]{4,3,2,1,0:T(8,128)(2,1)S(1)} %get-tuple-element.13), channel_id=1, source_target_pairs={{0,1},{1,0},{2,3},{3,2},{4,5},{5,4},{6,7},{7,6},{8,9},{9,8},{10,11... | collective-permute-start | bytes 786440 | tf_op jit(solution)/shard_map/ppermute | solution.py:250
  27.5 7.7 %collective-permute-start.5 = (bf16[1,2,32,1024]{3,2,1,0:T(8,128)(2,1)S(1)}, bf16[1,2,32,1024]{3,2,1,0:T(8,128)(2,1)S(1)}, u32[]{:S(2)}, u32[]{:S(2)}) collective-permute-start(bf16[1,2,32,1024]{3,2,1,0:T(8,128)(2,1)S(1)} %get-tuple-element.21), channel_id=1, source_target_pairs={{0,2},{2,0},{4,6},{6,4},{8,10},{10,8},{12,14},{14,12},{1,3},{3,1},... | collective-permute-start | bytes 393224 | tf_op jit(solution)/shard_map/ppermute | solution.py:253
  28.2 9.4 %collective-permute-start.6 = (bf16[1,2,32,1024]{3,2,1,0:T(8,128)(2,1)S(1)}, bf16[1,2,32,1024]{3,2,1,0:T(8,128)(2,1)S(1)}, u32[]{:S(2)}, u32[]{:S(2)}) collective-permute-start(bf16[1,2,32,1024]{3,2,1,0:T(8,128)(2,1)S(1)} %get-tuple-element.23), channel_id=1, source_target_pairs={{0,4},{2,6},{4,0},{6,2},{8,12},{10,14},{12,8},{14,10},{1,5},{3,7},... | collective-permute-start | bytes 393224 | tf_op jit(solution)/shard_map/ppermute | solution.py:253
  28.8 8.7 %collective-permute-start.7 = (bf16[1,2,32,1024]{3,2,1,0:T(8,128)(2,1)S(1)}, bf16[1,2,32,1024]{3,2,1,0:T(8,128)(2,1)S(1)}, u32[]{:S(2)}, u32[]{:S(2)}) collective-permute-start(bf16[1,2,32,1024]{3,2,1,0:T(8,128)(2,1)S(1)} %get-tuple-element.25), channel_id=1, source_target_pairs={{0,6},{2,4},{4,2},{6,0},{8,14},{10,12},{12,10},{14,8},{1,7},{3,5},... | collective-permute-start | bytes 393224 | tf_op jit(solution)/shard_map/ppermute | solution.py:253
  31.2 8.1 %collective-permute-start.1 = (bf16[1,2,32,1024]{3,2,1,0:T(8,128)(2,1)S(1)}, bf16[1,2,32,1024]{3,2,1,0:T(8,128)(2,1)S(1)}, u32[]{:S(2)}, u32[]{:S(2)}) collective-permute-start(bf16[1,2,32,1024]{3,2,1,0:T(8,128)(2,1)S(1)} %get-tuple-element.20), channel_id=1, source_target_pairs={{0,2},{2,0},{4,6},{6,4},{8,10},{10,8},{12,14},{14,12},{1,3},{3,1},... | collective-permute-start | bytes 393224 | tf_op jit(solution)/shard_map/ppermute | solution.py:253
  34.5 7.0 %collective-permute-start.2 = (bf16[1,2,32,1024]{3,2,1,0:T(8,128)(2,1)S(1)}, bf16[1,2,32,1024]{3,2,1,0:T(8,128)(2,1)S(1)}, u32[]{:S(2)}, u32[]{:S(2)}) collective-permute-start(bf16[1,2,32,1024]{3,2,1,0:T(8,128)(2,1)S(1)} %get-tuple-element.22), channel_id=1, source_target_pairs={{0,4},{2,6},{4,0},{6,2},{8,12},{10,14},{12,8},{14,10},{1,5},{3,7},... | collective-permute-start | bytes 393224 | tf_op jit(solution)/shard_map/ppermute | solution.py:253
  35.2 10.4 %collective-permute-start.3 = (bf16[1,2,32,1024]{3,2,1,0:T(8,128)(2,1)S(1)}, bf16[1,2,32,1024]{3,2,1,0:T(8,128)(2,1)S(1)}, u32[]{:S(2)}, u32[]{:S(2)}) collective-permute-start(bf16[1,2,32,1024]{3,2,1,0:T(8,128)(2,1)S(1)} %get-tuple-element.24), channel_id=1, source_target_pairs={{0,6},{2,4},{4,2},{6,0},{8,14},{10,12},{12,10},{14,8},{1,7},{3,5},... | collective-permute-start | bytes 393224 | tf_op jit(solution)/shard_map/ppermute | solution.py:253
  37.6 8.0 %collective-permute-start.8 = (bf16[1,2,32,1024]{3,2,1,0:T(8,128)(2,1)S(1)}, bf16[1,2,32,1024]{3,2,1,0:T(8,128)(2,1)S(1)}, u32[]{:S(2)}, u32[]{:S(2)}) collective-permute-start(bf16[1,2,32,1024]{3,2,1,0:T(8,128)(2,1)S(1)} %fusion), channel_id=1, source_target_pairs={{0,8},{2,10},{4,12},{6,14},{8,0},{10,2},{12,4},{14,6},{1,9},{3,11}... | collective-permute-start | bytes 393224 | tf_op jit(solution)/shard_map/ppermute | solution.py:253
  45.8 5.2 %collective-permute-start.9 = (bf16[1,32,1024]{2,1,0:T(8,128)(2,1)S(1)}, bf16[1,32,1024]{2,1,0:T(8,128)(2,1)S(1)}, u32[]{:S(2)}, u32[]{:S(2)}) collective-permute-start(bf16[1,32,1024]{2,1,0:T(8,128)(2,1)S(1)} %fusion.4), channel_id=1, source_target_pairs={{0,8},{2,10},{4,12},{6,14},{8,0},{10,2},{12,4},{14,6},{1,9},{3,11}... | collective-permute-start | bytes 196616 | tf_op jit(solution)/shard_map/ppermute | solution.py:253
  51.1 3.6 %collective-permute-start.12 = (bf16[64,1024]{1,0:T(8,128)(2,1)S(1)}, bf16[64,1024]{1,0:T(8,128)(2,1)S(1)}, u32[]{:S(2)}, u32[]{:S(2)}) collective-permute-start(bf16[64,1024]{1,0:T(8,128)(2,1)S(1)} %bitcast.42), channel_id=1, source_target_pairs={{0,1},{1,0},{2,3},{3,2},{4,5},{5,4},{6,7},{7,6},{8,9},{9,8},{10,11... | collective-permute-start | bytes 393224 | tf_op jit(solution)/shard_map/ppermute | solution.py:250
  51.1 7.3 %collective-permute-start.11 = (bf16[64,1024]{1,0:T(8,128)(2,1)S(1)}, bf16[64,1024]{1,0:T(8,128)(2,1)S(1)}, u32[]{:S(2)}, u32[]{:S(2)}) collective-permute-start(bf16[64,1024]{1,0:T(8,128)(2,1)S(1)} %bitcast.43), channel_id=1, source_target_pairs={{0,6},{2,4},{4,2},{6,0},{8,14},{10,12},{12,10},{14,8},{1,7},{3,5},... | collective-permute-start | bytes 393224 | tf_op jit(solution)/shard_map/ppermute | solution.py:253
  52.0 8.8 %collective-permute-start.13 = (bf16[64,1024]{1,0:T(8,128)(2,1)S(1)}, bf16[64,1024]{1,0:T(8,128)(2,1)S(1)}, u32[]{:S(2)}, u32[]{:S(2)}) collective-permute-start(bf16[64,1024]{1,0:T(8,128)(2,1)S(1)} %bitcast.44), channel_id=1, source_target_pairs={{0,4},{2,6},{4,0},{6,2},{8,12},{10,14},{12,8},{14,10},{1,5},{3,7},... | collective-permute-start | bytes 393224 | tf_op jit(solution)/shard_map/ppermute | solution.py:253
  52.7 8.1 %collective-permute-start.10 = (bf16[64,1024]{1,0:T(8,128)(2,1)S(1)}, bf16[64,1024]{1,0:T(8,128)(2,1)S(1)}, u32[]{:S(2)}, u32[]{:S(2)}) collective-permute-start(bf16[64,1024]{1,0:T(8,128)(2,1)S(1)} %bitcast.45), channel_id=1, source_target_pairs={{0,2},{2,0},{4,6},{6,4},{8,10},{10,8},{12,14},{14,12},{1,3},{3,1},... | collective-permute-start | bytes 393224 | tf_op jit(solution)/shard_map/ppermute | solution.py:253
  60.8 1.4 %collective-permute-start.15 = (bf16[64,1024]{1,0:T(8,128)(2,1)S(1)}, bf16[64,1024]{1,0:T(8,128)(2,1)S(1)}, u32[]{:S(2)}, u32[]{:S(2)}) collective-permute-start(bf16[64,1024]{1,0:T(8,128)(2,1)S(1)} %collective-permute-done.13.refs_1_), channel_id=1, source_target_pairs={{0,1},{1,0},{2,3},{3,2},{4,5},{5,4},{6,7},{7,6},{8,9},{9,8},{10,11... | collective-permute-start | bytes 393224 | tf_op jit(solution)/shard_map/ppermute | solution.py:250
  60.9 1.5 %collective-permute-start.14 = (bf16[64,1024]{1,0:T(8,128)(2,1)S(1)}, bf16[64,1024]{1,0:T(8,128)(2,1)S(1)}, u32[]{:S(2)}, u32[]{:S(2)}) collective-permute-start(bf16[64,1024]{1,0:T(8,128)(2,1)S(1)} %collective-permute-done.10.refs_0_), channel_id=1, source_target_pairs={{0,1},{1,0},{2,3},{3,2},{4,5},{5,4},{6,7},{7,6},{8,9},{9,8},{10,11... | collective-permute-start | bytes 393224 | tf_op jit(solution)/shard_map/ppermute | solution.py:250
  61.3 1.3 %collective-permute-start.16 = (bf16[64,1024]{1,0:T(8,128)(2,1)S(1)}, bf16[64,1024]{1,0:T(8,128)(2,1)S(1)}, u32[]{:S(2)}, u32[]{:S(2)}) collective-permute-start(bf16[64,1024]{1,0:T(8,128)(2,1)S(1)} %collective-permute-done.11.refs_0_), channel_id=1, source_target_pairs={{0,1},{1,0},{2,3},{3,2},{4,5},{5,4},{6,7},{7,6},{8,9},{9,8},{10,11... | collective-permute-start | bytes 393224 | tf_op jit(solution)/shard_map/ppermute | solution.py:250
